TPU v7x, 32 devices: a whole 2x2x4 slice. The times are simulated.
32 devices in a mesh: parts: 2 (over y), group: 4 (over z), tensor: 4 (over x, core).
Axes of the slice: x: 2, y: 2, z: 4, core: 2. Of those that a mesh axis runs over, the one named last changes fastest.
Arguments:
- queries: bfloat16 [512, 8192], P(('parts', 'group'), 'tensor'), parts along dimension 0, may hold values from -36 to 36
- keys: bfloat16 [512, 1024], P(('parts', 'group'), 'tensor'), parts along dimension 0, may hold values from -64 to 64
- values: bfloat16 [512, 1024], P(('parts', 'group'), 'tensor'), parts along dimension 0, may hold values from -6 to 6
- prefix_keys: bfloat16 [2048, 1024], P(('parts', 'group'), 'tensor'), parts along dimension 0, may hold values from -6 to 6
- prefix_values: bfloat16 [2048, 1024], P(('parts', 'group'), 'tensor'), parts along dimension 0, may hold values from -6 to 6
- spread: int32 [8], P('parts'), parts along dimension 0, may hold values from 0 to 3, as said below
- turn: int32 [8], P('parts'), parts along dimension 0, may hold values from 0 to 7
- new_blocks: int32 [8, 4], P('parts'), parts along dimension 0, may hold values from 1 to 2, as said below
- prefix_len: int32 [8, 4], P('parts'), parts along dimension 0, may hold values from 1 to 64, as said below
- owner: int32 [8, 4], P('parts'), parts along dimension 0, may hold values from 0 to 3, as said below
- page_start: int32 [8, 4], P('parts'), parts along dimension 0, may hold values from 0 to 6, as said below
Outputs:
- attention: bfloat16 [512, 8192], P(('parts', 'group'), 'tensor'), parts along dimension 0
- cache: bfloat16 [64, 2, 8, 1024], P(('parts', 'group'), None, 'tensor'), parts along dimension 0
There are 2 independent parts, one for each index of `parts`. A program takes and returns all parts, laid end to end along the dimension named above; each array names one. Nothing has to cross between parts.
Inputs may be any that keep to these rules, and one draw needn't show every extreme that they name: `spread`: A permutation of the numbers below 4. `new_blocks`: in every group one prompt has exactly 2 new blocks. `prefix_len`: in every group one prompt has exactly 64 cached tokens. `owner`: the prompts of one prefill group have different owners, and every decode group owns exactly one prompt of each index p. `page_start`: A multiple of 2; the prompts owned by one decode group start at different pages.
All inputs are finite; a program needn't handle non-finite values.
Results may differ from a plain program's by a relative error of at most 0.012.
The roundings to bfloat16 on the way count: a program that leaves them out, or rounds other values in their place, can miss the bound.
Values may be sent and summed in bfloat16 or wider, within the bound.
No kernel may reach another device: no remote copies, remote signals or barrier semaphores. Data moves between devices by JAX's collectives and lax.ppermute only.
A program may use at most 64 MiB of HBM per device.

v0:
```python
import functools
import math

import jax
import jax.numpy as jnp
import numpy as np
from jax import lax
from jax.experimental import pallas as pl
from jax.experimental.pallas import tpu as pltpu
from jax.sharding import PartitionSpec as P

HEAD = 128
BLOCK = 8
MAXP = 2
CTXP = 64

VMEM_LIMIT = 24 * 1024 * 1024

SMEM = pl.BlockSpec(memory_space=pltpu.SMEM)
VMEM = pl.BlockSpec(memory_space=pltpu.VMEM)
PROMPT, OFFSET, LIVE, CACHED, SOURCE, COLUMN, PLACE = range(7)
ANY = pl.BlockSpec(memory_space=pl.ANY)
HBM = pl.BlockSpec(memory_space=pltpu.HBM)


def rope_table():
    count = CTXP + MAXP * BLOCK
    half = HEAD // 2
    frequency = np.exp(np.arange(half) * (-2.0 * math.log(500000.0) / HEAD))
    angles = np.arange(count)[:, None] * frequency[None, :]
    cosine, sine = np.cos(angles), np.sin(angles)
    return (
        np.concatenate([cosine, cosine], axis=1).astype(np.float32),
        np.concatenate([-sine, sine], axis=1).astype(np.float32),
    )


def loop(count, body, unrolled=16):
    if count <= unrolled:
        for index in range(count):
            body(index)
    else:
        lax.fori_loop(0, count, lambda index, carry: (body(index), carry)[1], 0)


def turned(head_block, cosine, sine):
    return head_block * cosine + pltpu.roll(head_block, HEAD // 2, 1) * sine


def dispatch_kernel(
    groups, spread_in, turn_in, new_blocks_in, owner_in, queries_in, keys_in, values_in, *rest
):
    outs, handed, rest = rest[:groups], rest[groups : 2 * groups], rest[2 * groups :]
    spread, turn, new_blocks, owner, queries, keys, values, table, sem = rest
    own = lax.axis_index("group")
    slots, _, width_q = queries.shape
    width_k = keys.shape[2]
    capacity = slots // groups
    prompts = new_blocks.shape[1]
    copies = [
        pltpu.make_async_copy(source, target, sem.at[n])
        for n, (source, target) in enumerate(
            (
                (spread_in, spread),
                (turn_in, turn),
                (new_blocks_in, new_blocks),
                (owner_in, owner),
                (keys_in, keys),
                (values_in, values),
                (queries_in, queries),
            )
        )
    ]
    for copy in copies:
        copy.start()
    for copy in copies[:4]:
        copy.wait()

    def clear(n):
        table[n] = 0

    loop(groups * groups, clear)

    def column(c):
        target = lax.rem(own - spread[c] + groups, groups)

        def find(p, carry):
            start, holders = carry
            blocks = new_blocks[target, p]
            holders = [
                jnp.where((c + groups * n >= start) & (c + groups * n < start + blocks), owner[target, p], holder)
                for n, holder in enumerate(holders)
            ]
            return start + blocks, holders

        carry = (jnp.int32(0), [jnp.int32(-1)] * capacity)
        if prompts <= 8:
            for p in range(prompts):
                carry = find(p, carry)
        else:
            carry = lax.fori_loop(0, prompts, find, carry)
        for n, holder in enumerate(carry[1]):
            at = lax.rem(holder - own + groups, groups) * groups + target
            table[jnp.where(holder >= 0, at, groups * groups)] = lax.rem(c + groups * n + turn[own], slots)

    loop(groups, column)
    for copy in copies[4:]:
        copy.wait()
    for distance in range(groups):
        first_slot = column_of(spread, groups, distance) + turn[own]
        out = outs[distance]
        for step in range(capacity):
            source = lax.rem(first_slot + groups * step, slots)
            out[step, :, :width_q] = queries[source]
            out[step, :, width_q : width_q + width_k] = keys[source]
            out[step, :, width_q + width_k :] = values[source]

        def page(g):
            source = table[distance * groups + g]
            handed[distance][g, :, :width_k] = keys[source]
            handed[distance][g, :, width_k:] = values[source]

        loop(groups, page)


def column_of(spread, groups, distance):
    wanted = (groups - distance) % groups
    if groups <= 8:
        return sum(jnp.where(spread[c] == wanted, c, 0) for c in range(groups))
    return lax.fori_loop(
        0, groups, lambda c, found: jnp.where(spread[c] == wanted, c, found), jnp.int32(0)
    )


def make_plan(groups, own, spread, new_blocks, prefix_len, owner, page_start, plan):
    prompts = new_blocks.shape[1]
    slots = prompts * MAXP

    def clear(j):
        plan[PROMPT, j] = 0
        plan[OFFSET, j] = 0
        plan[LIVE, j] = 0
        plan[CACHED, j] = 0

    loop(slots, clear)

    def one(p, start):
        blocks = new_blocks[own, p]
        cached = prefix_len[own, p]
        for step in range(MAXP):
            at = jnp.where(step < blocks, start + step, slots)
            plan[PROMPT, at] = p
            plan[OFFSET, at] = cached + step * BLOCK
            plan[LIVE, at] = 1 + step
            plan[CACHED, at] = cached
        return start + blocks

    start = jnp.int32(0)
    if prompts <= 8:
        for p in range(prompts):
            start = one(p, start)
    else:
        lax.fori_loop(0, prompts, one, start)

    def of_group(g):
        def one(p, start):
            blocks = new_blocks[g, p]
            mine = owner[g, p] == own
            for step in range(MAXP):
                root = lax.rem(g + spread[lax.rem(start + step, groups)], groups)
                at = jnp.where(mine, page_start[g, p] + step, slots)
                away = lax.rem(own - root + groups, groups)
                plan[SOURCE, at] = jnp.where(step < blocks, away * groups + g, -1)
                plan[PLACE, at] = prefix_len[g, p] + step * BLOCK
            return start + blocks

        start = jnp.int32(0)
        if prompts <= 8:
            for p in range(prompts):
                start = one(p, start)
        else:
            lax.fori_loop(0, prompts, one, start)

    loop(groups, of_group)
    for distance in range(groups):
        plan[COLUMN, distance] = column_of(spread, groups, distance)


def pages_kernel(
    groups, tensors, spread, new_blocks, prefix_len, owner, page_start, cosine, sine, *rest
):
    chunks, rest = rest[:groups], rest[groups:]
    outs, (plan, blocks, rows) = rest[:tensors], rest[tensors:]
    own = lax.axis_index("group")
    own_tensor = lax.axis_index("tensor")
    pages = new_blocks.shape[1] * MAXP
    width_k = rows.shape[1]
    tokens = BLOCK // tensors
    for distance in range(groups):
        blocks[distance * groups : (distance + 1) * groups] = chunks[distance][...]
    make_plan(groups, own, spread, new_blocks, prefix_len, owner, page_start, plan)

    def assemble(page):
        source = plan[SOURCE, page]
        place = plan[PLACE, page]
        block = blocks[jnp.maximum(source, 0)].astype(jnp.float32)
        block = jnp.where(source >= 0, block, 0.0)
        cos = cosine[pl.ds(place, BLOCK), :]
        sin = sine[pl.ds(place, BLOCK), :]
        for first in range(0, width_k, HEAD):
            part = slice(first, first + HEAD)
            rows[pl.ds(pl.multiple_of(page * BLOCK, BLOCK), BLOCK), part] = turned(
                block[:, part], cos, sin
            )
        rows[pl.ds(pl.multiple_of((pages + page) * BLOCK, BLOCK), BLOCK), :] = block[:, width_k:]

    loop(pages, assemble)
    size = pages * 2 * tokens
    shape = (tensors * size, 2 * pages * BLOCK)
    row = lax.broadcasted_iota(jnp.int32, shape, 0)
    col = lax.broadcasted_iota(jnp.int32, shape, 1)
    share = lax.rem(row // size + own_tensor, tensors)
    kind, page = (row // tokens) % 2, (row // (2 * tokens)) % pages
    wanted = (kind * pages + page) * BLOCK + share * tokens + row % tokens
    pick = (col == wanted).astype(jnp.float32).astype(jnp.bfloat16)
    moved = jnp.dot(pick, rows[...].astype(jnp.bfloat16), preferred_element_type=jnp.float32)
    moved = moved.astype(jnp.bfloat16)
    for distance in range(tensors):
        outs[distance][...] = moved[distance * size : (distance + 1) * size]


def attention_kernel(groups, heads_q, heads_k, plan, prefix_keys, prefix_values, cosine, sine, *rest):
    arrived, (out, new_keys, new_values) = rest[:groups], rest[groups:]
    slots = out.shape[0]
    capacity = slots // groups
    ratio = heads_q // heads_k
    width_q = heads_q * HEAD
    width_k = heads_k * HEAD
    scale = math.log2(math.e) / math.sqrt(HEAD)
    span = CTXP + 2 * BLOCK
    lane = lax.broadcasted_iota(jnp.int32, (BLOCK, span), 1)
    token = lax.broadcasted_iota(jnp.int32, (BLOCK, span), 0)
    fresh = (lane >= CTXP + BLOCK) & (lane - (CTXP + BLOCK) <= token)
    before = (lane >= CTXP) & (lane < CTXP + BLOCK)

    blocks = []
    for distance in range(groups):
        first_slot = plan[COLUMN, distance]
        for step in range(capacity):
            j = first_slot + groups * step
            here = arrived[distance].at[step]
            cos = cosine[pl.ds(plan[OFFSET, j], BLOCK), :]
            sin = sine[pl.ds(plan[OFFSET, j], BLOCK), :]
            new_keys[j] = jnp.concatenate(
                [
                    turned(here[:, first : first + HEAD].astype(jnp.float32), cos, sin)
                    for first in range(width_q, width_q + width_k, HEAD)
                ],
                axis=1,
            )
            new_values[j] = here[:, width_q + width_k :].astype(jnp.float32)
            blocks.append((j, here, cos, sin))

    for at in range(0, len(blocks), 8):
        some = blocks[at : at + 8]
        for h in range(heads_k):
            part = slice(h * HEAD, (h + 1) * HEAD)
            scores = []
            for j, here, cos, sin in some:
                prev = jnp.maximum(j - 1, 0)
                region = pl.ds(pl.multiple_of(plan[PROMPT, j] * CTXP, CTXP), CTXP)
                mask = fresh | (lane < plan[CACHED, j]) & (lane < CTXP) | before & (plan[LIVE, j] == 2)
                new_key = jnp.concatenate([new_keys[prev, :, part], new_keys[j, :, part]], axis=0)
                key = jnp.concatenate([prefix_keys[region, part], new_key.astype(jnp.bfloat16)], axis=0)
                query = jnp.concatenate(
                    [
                        turned(here[:, n * HEAD : (n + 1) * HEAD].astype(jnp.float32), cos, sin)
                        for n in range(h * ratio, (h + 1) * ratio)
                    ],
                    axis=0,
                ).astype(jnp.bfloat16)
                score = lax.dot_general(
                    query, key, (((1,), (1,)), ((), ())), preferred_element_type=jnp.float32
                )
                scores.append(jnp.where(mask[None], score.reshape(ratio, BLOCK, span), -1e30))
            score = jnp.concatenate(scores, axis=0)
            top = jnp.max(score, axis=2, keepdims=True)
            powers = jnp.exp2((score - top) * scale)
            weights = powers * (1.0 / jnp.sum(powers, axis=2, keepdims=True))
            weights = weights.reshape(len(some), ratio * BLOCK, span).astype(jnp.bfloat16)
            for place, (j, here, cos, sin) in enumerate(some):
                prev = jnp.maximum(j - 1, 0)
                region = pl.ds(pl.multiple_of(plan[PROMPT, j] * CTXP, CTXP), CTXP)
                new_value = jnp.concatenate([new_values[prev, :, part], new_values[j, :, part]], axis=0)
                value = jnp.concatenate([prefix_values[region, part], new_value.astype(jnp.bfloat16)], axis=0)
                mixed = jnp.dot(weights[place], value, preferred_element_type=jnp.float32)
                mixed = jnp.where(plan[LIVE, j] > 0, mixed, 0.0)
                for n in range(ratio):
                    first = (h * ratio + n) * HEAD
                    out[j, :, first : first + HEAD] = mixed[n * BLOCK : (n + 1) * BLOCK].astype(
                        jnp.bfloat16
                    )


def cache_kernel(tensors, *rest):
    arrived, out = rest[:tensors], rest[tensors + 1]
    own_tensor = lax.axis_index("tensor")
    width_k = arrived[0].shape[1]
    for distance in range(tensors):
        sender = lax.rem(own_tensor - distance + tensors, tensors)
        at = pl.ds(pl.multiple_of(sender * width_k, HEAD), width_k)
        part = arrived[distance][...].astype(jnp.float32)
        out[:, :, at] = part.reshape(out.shape[0], out.shape[1], width_k).astype(jnp.bfloat16)


def in_hbm(operand):
    return pltpu.with_memory_space_constraint(operand, pltpu.HBM)


def shifted(chunks, axis):
    size = lax.axis_size(axis)
    return [chunks[0]] + [
        lax.ppermute(chunks[d], axis, [(i, (i + d) % size) for i in range(size)])
        for d in range(1, size)
    ]


def per_device(
    queries,
    keys,
    values,
    prefix_keys,
    prefix_values,
    spread,
    turn,
    new_blocks,
    prefix_len,
    owner,
    page_start,
):
    groups = lax.axis_size("group")
    tensors = lax.axis_size("tensor")
    width_q = queries.shape[1]
    width_k = keys.shape[1]
    heads_q = width_q // HEAD
    heads_k = width_k // HEAD
    slots = queries.shape[0] // BLOCK
    capacity = slots // groups
    prompts = new_blocks.shape[1]
    tokens = BLOCK // tensors
    pages = prompts * MAXP
    cosine, sine = (jnp.asarray(table) for table in rope_table())
    params = pltpu.CompilerParams(vmem_limit_bytes=VMEM_LIMIT)
    blocks_q = queries.reshape(slots, BLOCK, width_q)
    blocks_k = keys.reshape(slots, BLOCK, width_k)
    blocks_v = values.reshape(slots, BLOCK, width_k)

    chunk = jax.ShapeDtypeStruct((capacity, BLOCK, width_q + 2 * width_k), jnp.bfloat16)
    page_chunk = jax.ShapeDtypeStruct((groups, BLOCK, 2 * width_k), jnp.bfloat16)
    sent = pl.pallas_call(
        functools.partial(dispatch_kernel, groups),
        out_shape=[chunk] * groups + [page_chunk] * groups,
        in_specs=[HBM] * 7,
        out_specs=[VMEM] * (2 * groups),
        scratch_shapes=[
            *(pltpu.SMEM(array.shape, jnp.int32) for array in (spread, turn, new_blocks, owner)),
            *(pltpu.VMEM(array.shape, jnp.bfloat16) for array in (blocks_q, blocks_k, blocks_v)),
            pltpu.SMEM((groups * groups + 1,), jnp.int32),
            pltpu.SemaphoreType.DMA((7,)),
        ],
        compiler_params=params,
        name="dispatch",
    )(
        *(
            in_hbm(operand)
            for operand in (spread, turn, new_blocks, owner, blocks_q, blocks_k, blocks_v)
        )
    )
    arrived = shifted(sent[:groups], "group")
    handed = shifted(sent[groups:], "group")

    part = jax.ShapeDtypeStruct((pages * 2 * tokens, width_k), jnp.bfloat16)
    *finished, plan = pl.pallas_call(
        functools.partial(pages_kernel, groups, tensors),
        out_shape=[part] * tensors + [jax.ShapeDtypeStruct((7, max(slots, groups) + 1), jnp.int32)],
        in_specs=[SMEM] * 5 + [VMEM] * (2 + groups),
        out_specs=[VMEM] * tensors + [SMEM],
        compiler_params=params,
        scratch_shapes=[
            pltpu.VMEM((groups * groups, BLOCK, 2 * width_k), jnp.bfloat16),
            pltpu.VMEM((2 * pages * BLOCK, width_k), jnp.float32),
        ],
        name="finish_pages",
    )(spread, new_blocks, prefix_len, owner, page_start, cosine, sine, *handed)
    parts = shifted(finished, "tensor")

    attention = pl.pallas_call(
        functools.partial(attention_kernel, groups, heads_q, heads_k),
        out_shape=jax.ShapeDtypeStruct((slots, BLOCK, width_q), jnp.bfloat16),
        in_specs=[SMEM] + [VMEM] * (4 + groups),
        out_specs=VMEM,
        scratch_shapes=[pltpu.VMEM((slots, BLOCK, width_k), jnp.float32)] * 2,
        compiler_params=params,
        name="attention",
    )(plan, prefix_keys, prefix_values, cosine, sine, *arrived)

    cache = pl.pallas_call(
        functools.partial(cache_kernel, tensors),
        out_shape=jax.ShapeDtypeStruct((pages * 2, tokens, tensors * width_k), jnp.bfloat16),
        in_specs=[VMEM] * tensors + [ANY],
        out_specs=VMEM,
        compiler_params=params,
        name="place_pages",
    )(*parts, in_hbm(attention))
    return (
        attention.reshape(slots * BLOCK, width_q),
        cache.reshape(pages, 2, tokens, tensors * width_k),
    )


def solution(mesh):
    return jax.shard_map(
        per_device,
        mesh=mesh,
        in_specs=(
            P(("parts", "group"), "tensor"),
            P(("parts", "group"), "tensor"),
            P(("parts", "group"), "tensor"),
            P(("parts", "group"), "tensor"),
            P(("parts", "group"), "tensor"),
            P("parts"),
            P("parts"),
            P("parts", None),
            P("parts", None),
            P("parts", None),
            P("parts", None),
        ),
        out_specs=(P(("parts", "group"), "tensor"), P(("parts", "group"), None, "tensor", None)),
        check_vma=False,
    )
```

profile of v0, /device:TPU:0, one launch (start us, length us, event | category | flops | bytes accessed | tf_op | source)
XLA Modules:
  0.0 25.3 jit_solution(7562132862334213721)
XLA Ops:
  0.6 0.0 copy-start
  0.6 0.0 copy-start.1
  0.7 1.2 %dispatch.1 = (bf16[2,8,2560]{2,1,0:T(8,128)(2,1)S(1)}, bf16[2,8,2560]{2,1,0:T(8,128)(2,1)S(1)}, bf16[2,8,2560]{2,1,0:T(8,128)(2,1)S(1)}, bf16[2,8,2560]{2,1,0:T...) custom-call(s32[4]{0:T(128)} %spread.1, ...), custom_call_target="tpu_custom_call" | custom-call | tf_op jit(solution)/shard_map/dispatch/pallas_call | solution.py:360
  1.9 0.0 copy-start.2
  1.9 3.1 %collective-permute-start.3 = (bf16[2,8,2560]{2,1,0:T(8,128)(2,1)S(1)}, bf16[2,8,2560]{2,1,0:T(8,128)(2,1)S(1)}, u32[]{:S(2)}, u32[]{:S(2)}) collective-permute-start(bf16[2,8,2560]{2,1,0:T(8,128)(2,1)S(1)} %get-tuple-element.21), channel_id=1, source_target_pairs={{0,4},{4,8},{8,12},{12,0},{1,5},{5,9},{9,13},{13,1},{2,6},{6,10},{... | collective-permute-start | bytes 245768 | tf_op jit(solution)/shard_map/ppermute | solution.py:323
  5.0 1.6 %collective-permute-start = (bf16[4,8,512]{2,1,0:T(8,128)(2,1)S(1)}, bf16[4,8,512]{2,1,0:T(8,128)(2,1)S(1)}, u32[]{:S(2)}, u32[]{:S(2)}) collective-permute-start(bf16[4,8,512]{2,1,0:T(8,128)(2,1)S(1)} %get-tuple-element.16), channel_id=1, source_target_pairs={{0,4},{4,8},{8,12},{12,0},{1,5},{5,9},{9,13},{13,1},{2,6},{6,10},{... | collective-permute-start | bytes 98312 | tf_op jit(solution)/shard_map/ppermute | solution.py:323
  6.6 1.1 %collective-permute-start.4 = (bf16[2,8,2560]{2,1,0:T(8,128)(2,1)S(1)}, bf16[2,8,2560]{2,1,0:T(8,128)(2,1)S(1)}, u32[]{:S(2)}, u32[]{:S(2)}) collective-permute-start(bf16[2,8,2560]{2,1,0:T(8,128)(2,1)S(1)} %get-tuple-element.22), channel_id=1, source_target_pairs={{0,8},{4,12},{8,0},{12,4},{1,9},{5,13},{9,1},{13,5},{2,10},{6,14},... | collective-permute-start | bytes 245768 | tf_op jit(solution)/shard_map/ppermute | solution.py:323
  7.7 2.9 %collective-permute-start.5 = (bf16[2,8,2560]{2,1,0:T(8,128)(2,1)S(1)}, bf16[2,8,2560]{2,1,0:T(8,128)(2,1)S(1)}, u32[]{:S(2)}, u32[]{:S(2)}) collective-permute-start(bf16[2,8,2560]{2,1,0:T(8,128)(2,1)S(1)} %get-tuple-element.23), channel_id=1, source_target_pairs={{0,12},{4,0},{8,4},{12,8},{1,13},{5,1},{9,5},{13,9},{2,14},{6,2},{... | collective-permute-start | bytes 245768 | tf_op jit(solution)/shard_map/ppermute | solution.py:323
  10.5 0.3 %collective-permute-start.1 = (bf16[4,8,512]{2,1,0:T(8,128)(2,1)S(1)}, bf16[4,8,512]{2,1,0:T(8,128)(2,1)S(1)}, u32[]{:S(2)}, u32[]{:S(2)}) collective-permute-start(bf16[4,8,512]{2,1,0:T(8,128)(2,1)S(1)} %get-tuple-element.17), channel_id=1, source_target_pairs={{0,8},{4,12},{8,0},{12,4},{1,9},{5,13},{9,1},{13,5},{2,10},{6,14},... | collective-permute-start | bytes 98312 | tf_op jit(solution)/shard_map/ppermute | solution.py:323
  10.9 0.3 %collective-permute-done.rest_1_ = bf16[4,8,512]{2,1,0:T(8,128)(2,1)S(1)} collective-permute-done((bf16[4,8,512]{2,1,0:T(8,128)(2,1)S(1)}, bf16[4,8,512]{2,1,0:T(8,128)(2,1)S(1)}, u32[]{:S(2)}, u32[]{:S(2)}) %collective-permute-start) | collective-permute-done | bytes 32800 | tf_op jit(solution)/shard_map/ppermute | solution.py:323
  11.2 0.9 %collective-permute-start.2 = (bf16[4,8,512]{2,1,0:T(8,128)(2,1)S(1)}, bf16[4,8,512]{2,1,0:T(8,128)(2,1)S(1)}, u32[]{:S(2)}, u32[]{:S(2)}) collective-permute-start(bf16[4,8,512]{2,1,0:T(8,128)(2,1)S(1)} %get-tuple-element.18), channel_id=1, source_target_pairs={{0,12},{4,0},{8,4},{12,8},{1,13},{5,1},{9,5},{13,9},{2,14},{6,2},{... | collective-permute-start | bytes 98312 | tf_op jit(solution)/shard_map/ppermute | solution.py:323
  12.1 5.1 %collective-permute-done.1.rest_2_ = bf16[4,8,512]{2,1,0:T(8,128)(2,1)S(1)} collective-permute-done((bf16[4,8,512]{2,1,0:T(8,128)(2,1)S(1)}, bf16[4,8,512]{2,1,0:T(8,128)(2,1)S(1)}, u32[]{:S(2)}, u32[]{:S(2)}) %collective-permute-start.1) | collective-permute-done | bytes 32800 | tf_op jit(solution)/shard_map/ppermute | solution.py:323
  17.2 0.0 collective-permute-done.2.rest_3_
  17.3 1.8 %finish_pages.1 = (bf16[32,256]{1,0:T(8,128)(2,1)S(1)}, bf16[32,256]{1,0:T(8,128)(2,1)S(1)}, bf16[32,256]{1,0:T(8,128)(2,1)S(1)}, bf16[32,256]{1,0:T(8,128)(2,1)S(1)}, s32[7,9]{1,0:T(8,128)S(1)}) custom-call(s32[4]{0:T(128)S(1)} %copy-done.8, s32[4,4]{1,0:T(4,128)S(1)} %copy-done.4, s32[4,4]{1,0:T(4,128)S(1)} %copy-done.6, s32[4,4]{1,0:T(4,128)S(1)} %copy-done.5, ...), custom_call_target="tpu_custom_call" | custom-call | tf_op jit(solution)/shard_map/finish_pages/pallas_call | solution.py:383
  19.1 0.1 collective-permute-start.6
  19.1 1.8 %collective-permute-start.7 = (bf16[32,256]{1,0:T(8,128)(2,1)S(1)}, bf16[32,256]{1,0:T(8,128)(2,1)S(1)}, u32[]{:S(2)}, u32[]{:S(2)}) collective-permute-start(bf16[32,256]{1,0:T(8,128)(2,1)S(1)} %get-tuple-element.26), channel_id=1, source_target_pairs={{0,2},{1,3},{2,0},{3,1},{4,6},{5,7},{6,4},{7,5},{8,10},{9,11},{10,... | collective-permute-start | bytes 49160 | tf_op jit(solution)/shard_map/ppermute | solution.py:323
  20.9 0.0 collective-permute-done.3.rest_1_
  20.9 1.4 %collective-permute-start.8 = (bf16[32,256]{1,0:T(8,128)(2,1)S(1)}, bf16[32,256]{1,0:T(8,128)(2,1)S(1)}, u32[]{:S(2)}, u32[]{:S(2)}) collective-permute-start(bf16[32,256]{1,0:T(8,128)(2,1)S(1)} %get-tuple-element.27), channel_id=1, source_target_pairs={{0,3},{1,0},{2,1},{3,2},{4,7},{5,4},{6,5},{7,6},{8,11},{9,8},{10,9... | collective-permute-start | bytes 49160 | tf_op jit(solution)/shard_map/ppermute | solution.py:323
  22.3 0.0 collective-permute-done.4.rest_2_
  22.3 0.0 collective-permute-done.5.rest_3_
  22.3 2.3 %attention.1.rest_4_ = bf16[8,8,2048]{2,1,0:T(8,128)(2,1)} custom-call(s32[7,9]{1,0:T(8,128)S(1)} %get-tuple-element.19.plan, bf16[256,256]{1,0:T(8,128)(2,1)S(1)} %copy-done.2, bf16[256,256]{1,0:T(8,128)(2,1)S(1)} %copy-done.3, f32[80,128]{1,0:T(8,128)S(1)} %copy-done.1, f32[80,128]{1,0:T(8,128)S(1)} %copy-done, ...), custom_call_target="tpu_custom_call" | custom-call | tf_op jit(solution)/shard_map/attention/pallas_call | solution.py:397
  24.6 0.0 collective-permute-done.7.rest_2_
  24.6 0.0 collective-permute-done.8.rest_3_
  24.6 0.7 %place_pages.1 = bf16[16,2,1024]{2,1,0:T(2,128)(2,1)} custom-call(bf16[32,256]{1,0:T(8,128)(2,1)S(1)} %get-tuple-element.24.rest_0_, bf16[32,256]{1,0:T(8,128)(2,1)S(1)} %collective-permute-done.6.rest_1_, bf16[32,256]{1,0:T(8,128)(2,1)S(1)} %collective-permute-done.7.rest_2_, bf16[32,256]{1,0:T(8,128)(2,1)S(1)} %collective-permute-done.8.rest_3_, ...), custom_call_target="tpu_custom_call" | custom-call | tf_op jit(solution)/shard_map/place_pages/pallas_call | solution.py:407
  (16 shorter events, 0.0 us)
Async XLA Ops:
  0.6 16.6 %copy-start = (f32[80,128]{1,0:T(8,128)S(1)}, f32[80,128]{1,0:T(8,128)}, u32[]{:S(2)}) copy-start(f32[80,128]{1,0:T(8,128)} %constant.5.clone.sine) | copy-start | bytes 122884
  0.6 16.6 %copy-start.1 = (f32[80,128]{1,0:T(8,128)S(1)}, f32[80,128]{1,0:T(8,128)}, u32[]{:S(2)}) copy-start(f32[80,128]{1,0:T(8,128)} %constant.4.clone.cosine) | copy-start | bytes 122884
  0.7 16.6 %copy-start.4 = (s32[4,4]{1,0:T(4,128)S(1)}, s32[4,4]{1,0:T(4,128)}, u32[]{:S(2)}) copy-start(s32[4,4]{1,0:T(4,128)} %new_blocks.1) | copy-start | bytes 196
  0.7 16.6 %copy-start.5 = (s32[4,4]{1,0:T(4,128)S(1)}, s32[4,4]{1,0:T(4,128)}, u32[]{:S(2)}) copy-start(s32[4,4]{1,0:T(4,128)} %owner.1) | copy-start | bytes 196
  0.7 16.6 %copy-start.6 = (s32[4,4]{1,0:T(4,128)S(1)}, s32[4,4]{1,0:T(4,128)}, u32[]{:S(2)}) copy-start(s32[4,4]{1,0:T(4,128)} %prefix_len.1) | copy-start | bytes 196
  0.7 16.6 %copy-start.7 = (s32[4,4]{1,0:T(4,128)S(1)}, s32[4,4]{1,0:T(4,128)}, u32[]{:S(2)}) copy-start(s32[4,4]{1,0:T(4,128)} %page_start.1) | copy-start | bytes 196
  0.7 16.6 %copy-start.8 = (s32[4]{0:T(128)S(1)}, s32[4]{0:T(128)}, u32[]{:S(2)}) copy-start(s32[4]{0:T(128)} %spread.1) | copy-start | bytes 52
  0.7 21.6 %copy-start.3 = (bf16[256,256]{1,0:T(8,128)(2,1)S(1)}, bf16[256,256]{1,0:T(8,128)(2,1)}, u32[]{:S(2)}) copy-start(bf16[256,256]{1,0:T(8,128)(2,1)} %prefix_values.1) | copy-start | bytes 393220
  1.9 20.4 %copy-start.2 = (bf16[256,256]{1,0:T(8,128)(2,1)S(1)}, bf16[256,256]{1,0:T(8,128)(2,1)}, u32[]{:S(2)}) copy-start(bf16[256,256]{1,0:T(8,128)(2,1)} %prefix_keys.1) | copy-start | bytes 393220
  1.9 19.0 %collective-permute-start.3 = (bf16[2,8,2560]{2,1,0:T(8,128)(2,1)S(1)}, bf16[2,8,2560]{2,1,0:T(8,128)(2,1)S(1)}, u32[]{:S(2)}, u32[]{:S(2)}) collective-permute-start(bf16[2,8,2560]{2,1,0:T(8,128)(2,1)S(1)} %get-tuple-element.21), channel_id=1, source_target_pairs={{0,4},{4,8},{8,12},{12,0},{1,5},{5,9},{9,13},{13,1},{2,6},{6,10},{... | collective-permute-start | bytes 245768 | tf_op jit(solution)/shard_map/ppermute | solution.py:323
  5.0 6.2 %collective-permute-start = (bf16[4,8,512]{2,1,0:T(8,128)(2,1)S(1)}, bf16[4,8,512]{2,1,0:T(8,128)(2,1)S(1)}, u32[]{:S(2)}, u32[]{:S(2)}) collective-permute-start(bf16[4,8,512]{2,1,0:T(8,128)(2,1)S(1)} %get-tuple-element.16), channel_id=1, source_target_pairs={{0,4},{4,8},{8,12},{12,0},{1,5},{5,9},{9,13},{13,1},{2,6},{6,10},{... | collective-permute-start | bytes 98312 | tf_op jit(solution)/shard_map/ppermute | solution.py:323
  6.6 15.7 %collective-permute-start.4 = (bf16[2,8,2560]{2,1,0:T(8,128)(2,1)S(1)}, bf16[2,8,2560]{2,1,0:T(8,128)(2,1)S(1)}, u32[]{:S(2)}, u32[]{:S(2)}) collective-permute-start(bf16[2,8,2560]{2,1,0:T(8,128)(2,1)S(1)} %get-tuple-element.22), channel_id=1, source_target_pairs={{0,8},{4,12},{8,0},{12,4},{1,9},{5,13},{9,1},{13,5},{2,10},{6,14},... | collective-permute-start | bytes 245768 | tf_op jit(solution)/shard_map/ppermute | solution.py:323
  7.7 14.6 %collective-permute-start.5 = (bf16[2,8,2560]{2,1,0:T(8,128)(2,1)S(1)}, bf16[2,8,2560]{2,1,0:T(8,128)(2,1)S(1)}, u32[]{:S(2)}, u32[]{:S(2)}) collective-permute-start(bf16[2,8,2560]{2,1,0:T(8,128)(2,1)S(1)} %get-tuple-element.23), channel_id=1, source_target_pairs={{0,12},{4,0},{8,4},{12,8},{1,13},{5,1},{9,5},{13,9},{2,14},{6,2},{... | collective-permute-start | bytes 245768 | tf_op jit(solution)/shard_map/ppermute | solution.py:323
  10.5 6.7 %collective-permute-start.1 = (bf16[4,8,512]{2,1,0:T(8,128)(2,1)S(1)}, bf16[4,8,512]{2,1,0:T(8,128)(2,1)S(1)}, u32[]{:S(2)}, u32[]{:S(2)}) collective-permute-start(bf16[4,8,512]{2,1,0:T(8,128)(2,1)S(1)} %get-tuple-element.17), channel_id=1, source_target_pairs={{0,8},{4,12},{8,0},{12,4},{1,9},{5,13},{9,1},{13,5},{2,10},{6,14},... | collective-permute-start | bytes 98312 | tf_op jit(solution)/shard_map/ppermute | solution.py:323
  11.2 6.0 %collective-permute-start.2 = (bf16[4,8,512]{2,1,0:T(8,128)(2,1)S(1)}, bf16[4,8,512]{2,1,0:T(8,128)(2,1)S(1)}, u32[]{:S(2)}, u32[]{:S(2)}) collective-permute-start(bf16[4,8,512]{2,1,0:T(8,128)(2,1)S(1)} %get-tuple-element.18), channel_id=1, source_target_pairs={{0,12},{4,0},{8,4},{12,8},{1,13},{5,1},{9,5},{13,9},{2,14},{6,2},{... | collective-permute-start | bytes 98312 | tf_op jit(solution)/shard_map/ppermute | solution.py:323
  19.1 5.6 %collective-permute-start.6 = (bf16[32,256]{1,0:T(8,128)(2,1)S(1)}, bf16[32,256]{1,0:T(8,128)(2,1)S(1)}, u32[]{:S(2)}, u32[]{:S(2)}) collective-permute-start(bf16[32,256]{1,0:T(8,128)(2,1)S(1)} %get-tuple-element.25), channel_id=1, source_target_pairs={{0,1},{1,2},{2,3},{3,0},{4,5},{5,6},{6,7},{7,4},{8,9},{9,10},{10,1... | collective-permute-start | bytes 49160 | tf_op jit(solution)/shard_map/ppermute | solution.py:323
  19.1 5.5 %collective-permute-start.7 = (bf16[32,256]{1,0:T(8,128)(2,1)S(1)}, bf16[32,256]{1,0:T(8,128)(2,1)S(1)}, u32[]{:S(2)}, u32[]{:S(2)}) collective-permute-start(bf16[32,256]{1,0:T(8,128)(2,1)S(1)} %get-tuple-element.26), channel_id=1, source_target_pairs={{0,2},{1,3},{2,0},{3,1},{4,6},{5,7},{6,4},{7,5},{8,10},{9,11},{10,... | collective-permute-start | bytes 49160 | tf_op jit(solution)/shard_map/ppermute | solution.py:323
  20.9 3.7 %collective-permute-start.8 = (bf16[32,256]{1,0:T(8,128)(2,1)S(1)}, bf16[32,256]{1,0:T(8,128)(2,1)S(1)}, u32[]{:S(2)}, u32[]{:S(2)}) collective-permute-start(bf16[32,256]{1,0:T(8,128)(2,1)S(1)} %get-tuple-element.27), channel_id=1, source_target_pairs={{0,3},{1,0},{2,1},{3,2},{4,7},{5,4},{6,5},{7,6},{8,11},{9,8},{10,9... | collective-permute-start | bytes 49160 | tf_op jit(solution)/shard_map/ppermute | solution.py:323
where the time goes:
time: 25.5 us; the launch traced here: 25.3 us
  starting transfers between devices  13 us (51%)
  Pallas kernels  6.02 us (24%)
  waiting for transfers between devices  5.47 us (21%)
  between operations  0.79 us (3%)
    ppermute x9, starting transfers between devices, shifted(): lax.ppermute(chunks[d], axis, [(i, (i + d) % size) for i in range(size)])  13 us
    ppermute x9, waiting for transfers between devices, shifted(): lax.ppermute(chunks[d], axis, [(i, (i + d) % size) for i in range(size)])  5.47 us
    pallas_call x1, Pallas kernels, per_device(): pl.pallas_call(functools.partial(attention_kernel, groups, heads_q, heads...  2.34 us
    pallas_call x1, Pallas kernels, per_device(): pl.pallas_call(functools.partial(pages_kernel, groups, tensors), out_shap...  1.8 us
    pallas_call x1, Pallas kernels, per_device(): pl.pallas_call(functools.partial(dispatch_kernel, groups), out_shape=[chu...  1.19 us
    pallas_call x1, Pallas kernels, per_device(): pl.pallas_call(functools.partial(cache_kernel, tensors), out_shape=jax.Sh...  0.69 us
  transfers between devices with their start and end apart: 9, of which 2 were waited for; matrix products, arithmetic and copies ran while one was open for 0% of the time, Pallas kernels for 16%

commit v1 on v0

--- a/solution.py
+++ b/solution.py
@@ -317,6 +317,18 @@
     return pltpu.with_memory_space_constraint(operand, pltpu.HBM)
 
 
+def after(arrays, others):
+    return pl.pallas_call(
+        lambda *refs: None,
+        out_shape=[jax.ShapeDtypeStruct(array.shape, array.dtype) for array in arrays],
+        in_specs=[ANY] * (len(arrays) + len(others)),
+        out_specs=[ANY] * len(arrays),
+        input_output_aliases={n: n for n in range(len(arrays))},
+        compiler_params=pltpu.CompilerParams(vmem_limit_bytes=VMEM_LIMIT),
+        name="hold",
+    )(*arrays, *others)
+
+
 def shifted(chunks, axis):
     size = lax.axis_size(axis)
     return [chunks[0]] + [
@@ -376,8 +388,8 @@
             for operand in (spread, turn, new_blocks, owner, blocks_q, blocks_k, blocks_v)
         )
     )
-    arrived = shifted(sent[:groups], "group")
     handed = shifted(sent[groups:], "group")
+    arrived = shifted([sent[0], *after(sent[1:groups], handed[1:])], "group")
 
     part = jax.ShapeDtypeStruct((pages * 2 * tokens, width_k), jnp.bfloat16)
     *finished, plan = pl.pallas_call(

time: 25.5 us -> 23.4 us (0.918)
  waiting for transfers between devices: 5.47 us -> 2.63 us
  starting transfers between devices: 13 us -> 13.9 us
    ppermute x9, waiting for transfers between devices: 5.47 us -> 2.63 us  [shifted(): lax.ppermute(chunks[d], axis, [(i, (i + d) % size) for i in range(size)])]
    ppermute x9, starting transfers between devices: 13 us -> 13.9 us  [shifted(): lax.ppermute(chunks[d], axis, [(i, (i + d) % size) for i in range(size)])]
  transfers between devices with their start and end apart: 9 -> 9, of which waited for: 2 -> 2; matrix products, arithmetic and copies ran while one was open for 0% -> 0% of each run, Pallas kernels for 16% -> 18%
where the time goes in v1:
time: 23.4 us; the launch traced here: 23.3 us
  starting transfers between devices  13.9 us (59%)
  Pallas kernels  5.95 us (25%)
  waiting for transfers between devices  2.63 us (11%)
  between operations  0.75 us (3%)
    ppermute x9, starting transfers between devices, shifted(): lax.ppermute(chunks[d], axis, [(i, (i + d) % size) for i in range(size)])  13.9 us
    ppermute x9, waiting for transfers between devices, shifted(): lax.ppermute(chunks[d], axis, [(i, (i + d) % size) for i in range(size)])  2.63 us
    pallas_call x1, Pallas kernels, per_device(): pl.pallas_call(functools.partial(attention_kernel, groups, heads_q, heads...  2.34 us
    pallas_call x1, Pallas kernels, per_device(): pl.pallas_call(functools.partial(pages_kernel, groups, tensors), out_shap...  1.8 us
    pallas_call x1, Pallas kernels, per_device(): pl.pallas_call(functools.partial(dispatch_kernel, groups), out_shape=[chu...  1.12 us
    pallas_call x1, Pallas kernels, per_device(): pl.pallas_call(functools.partial(cache_kernel, tensors), out_shape=jax.Sh...  0.69 us
  transfers between devices with their start and end apart: 9, of which 2 were waited for; matrix products, arithmetic and copies ran while one was open for 0% of the time, Pallas kernels for 18%

profile of v1, /device:TPU:0, one launch (start us, length us, event | category | flops | bytes accessed | tf_op | source)
XLA Modules:
  0.0 23.3 jit_solution(13578771919651218731)
XLA Ops:
  0.6 1.1 %dispatch.1 = (bf16[2,8,2560]{2,1,0:T(8,128)(2,1)S(1)}, bf16[2,8,2560]{2,1,0:T(8,128)(2,1)S(1)}, bf16[2,8,2560]{2,1,0:T(8,128)(2,1)S(1)}, bf16[2,8,2560]{2,1,0:T...) custom-call(s32[4]{0:T(128)} %spread.1, ...), custom_call_target="tpu_custom_call" | custom-call | tf_op jit(solution)/shard_map/dispatch/pallas_call | solution.py:372
  1.8 3.1 %collective-permute-start = (bf16[4,8,512]{2,1,0:T(8,128)(2,1)S(1)}, bf16[4,8,512]{2,1,0:T(8,128)(2,1)S(1)}, u32[]{:S(2)}, u32[]{:S(2)}) collective-permute-start(bf16[4,8,512]{2,1,0:T(8,128)(2,1)S(1)} %get-tuple-element.19), channel_id=1, source_target_pairs={{0,4},{4,8},{8,12},{12,0},{1,5},{5,9},{9,13},{13,1},{2,6},{6,10},{... | collective-permute-start | bytes 98312 | tf_op jit(solution)/shard_map/ppermute | solution.py:335
  4.8 2.6 %collective-permute-start.1 = (bf16[4,8,512]{2,1,0:T(8,128)(2,1)S(1)}, bf16[4,8,512]{2,1,0:T(8,128)(2,1)S(1)}, u32[]{:S(2)}, u32[]{:S(2)}) collective-permute-start(bf16[4,8,512]{2,1,0:T(8,128)(2,1)S(1)} %get-tuple-element.20), channel_id=1, source_target_pairs={{0,8},{4,12},{8,0},{12,4},{1,9},{5,13},{9,1},{13,5},{2,10},{6,14},... | collective-permute-start | bytes 98312 | tf_op jit(solution)/shard_map/ppermute | solution.py:335
  7.4 1.3 %collective-permute-start.2 = (bf16[4,8,512]{2,1,0:T(8,128)(2,1)S(1)}, bf16[4,8,512]{2,1,0:T(8,128)(2,1)S(1)}, u32[]{:S(2)}, u32[]{:S(2)}) collective-permute-start(bf16[4,8,512]{2,1,0:T(8,128)(2,1)S(1)} %get-tuple-element.21), channel_id=1, source_target_pairs={{0,12},{4,0},{8,4},{12,8},{1,13},{5,1},{9,5},{13,9},{2,14},{6,2},{... | collective-permute-start | bytes 98312 | tf_op jit(solution)/shard_map/ppermute | solution.py:335
  8.8 0.0 collective-permute-done.rest_1_.refs_3_
  8.8 1.2 %collective-permute-done.1.rest_2_.refs_4_ = bf16[4,8,512]{2,1,0:T(8,128)(2,1)S(1)} collective-permute-done((bf16[4,8,512]{2,1,0:T(8,128)(2,1)S(1)}, bf16[4,8,512]{2,1,0:T(8,128)(2,1)S(1)}, u32[]{:S(2)}, u32[]{:S(2)}) %collective-permute-start.1) | collective-permute-done | bytes 32800 | tf_op jit(solution)/shard_map/ppermute | solution.py:335
  10.0 1.3 %collective-permute-done.2.rest_3_.refs_5_ = bf16[4,8,512]{2,1,0:T(8,128)(2,1)S(1)} collective-permute-done((bf16[4,8,512]{2,1,0:T(8,128)(2,1)S(1)}, bf16[4,8,512]{2,1,0:T(8,128)(2,1)S(1)}, u32[]{:S(2)}, u32[]{:S(2)}) %collective-permute-start.2) | collective-permute-done | bytes 32800 | tf_op jit(solution)/shard_map/ppermute | solution.py:335
  11.3 0.0 copy-start.6
  11.4 0.0 copy-start.7
  11.4 0.0 copy-start.8
  11.4 0.0 copy-start.3
  11.4 0.0 copy-start.2
  11.4 0.3 %collective-permute-start.3 = (bf16[2,8,2560]{2,1,0:T(8,128)(2,1)S(1)}, bf16[2,8,2560]{2,1,0:T(8,128)(2,1)S(1)}, u32[]{:S(2)}, u32[]{:S(2)}) collective-permute-start(bf16[2,8,2560]{2,1,0:T(8,128)(2,1)S(1)} %get-tuple-element.27), channel_id=1, source_target_pairs={{0,4},{4,8},{8,12},{12,0},{1,5},{5,9},{9,13},{13,1},{2,6},{6,10},{... | collective-permute-start | bytes 245768 | tf_op jit(solution)/shard_map/ppermute | solution.py:335
  11.7 3.5 %collective-permute-start.4 = (bf16[2,8,2560]{2,1,0:T(8,128)(2,1)S(1)}, bf16[2,8,2560]{2,1,0:T(8,128)(2,1)S(1)}, u32[]{:S(2)}, u32[]{:S(2)}) collective-permute-start(bf16[2,8,2560]{2,1,0:T(8,128)(2,1)S(1)} %get-tuple-element.28), channel_id=1, source_target_pairs={{0,8},{4,12},{8,0},{12,4},{1,9},{5,13},{9,1},{13,5},{2,10},{6,14},... | collective-permute-start | bytes 245768 | tf_op jit(solution)/shard_map/ppermute | solution.py:335
  15.2 0.1 collective-permute-start.5
  15.4 1.8 %finish_pages.1 = (bf16[32,256]{1,0:T(8,128)(2,1)S(1)}, bf16[32,256]{1,0:T(8,128)(2,1)S(1)}, bf16[32,256]{1,0:T(8,128)(2,1)S(1)}, bf16[32,256]{1,0:T(8,128)(2,1)S(1)}, s32[7,9]{1,0:T(8,128)S(1)}) custom-call(s32[4]{0:T(128)S(1)} %copy-done.8, s32[4,4]{1,0:T(4,128)S(1)} %copy-done.4, s32[4,4]{1,0:T(4,128)S(1)} %copy-done.6, s32[4,4]{1,0:T(4,128)S(1)} %copy-done.5, ...), custom_call_target="tpu_custom_call" | custom-call | tf_op jit(solution)/shard_map/finish_pages/pallas_call | solution.py:395
  17.2 0.1 collective-permute-start.6
  17.2 1.6 %collective-permute-start.7 = (bf16[32,256]{1,0:T(8,128)(2,1)S(1)}, bf16[32,256]{1,0:T(8,128)(2,1)S(1)}, u32[]{:S(2)}, u32[]{:S(2)}) collective-permute-start(bf16[32,256]{1,0:T(8,128)(2,1)S(1)} %get-tuple-element.32), channel_id=1, source_target_pairs={{0,2},{1,3},{2,0},{3,1},{4,6},{5,7},{6,4},{7,5},{8,10},{9,11},{10,... | collective-permute-start | bytes 49160 | tf_op jit(solution)/shard_map/ppermute | solution.py:335
  18.8 1.4 %collective-permute-start.8 = (bf16[32,256]{1,0:T(8,128)(2,1)S(1)}, bf16[32,256]{1,0:T(8,128)(2,1)S(1)}, u32[]{:S(2)}, u32[]{:S(2)}) collective-permute-start(bf16[32,256]{1,0:T(8,128)(2,1)S(1)} %get-tuple-element.33), channel_id=1, source_target_pairs={{0,3},{1,0},{2,1},{3,2},{4,7},{5,4},{6,5},{7,6},{8,11},{9,8},{10,9... | collective-permute-start | bytes 49160 | tf_op jit(solution)/shard_map/ppermute | solution.py:335
  20.2 0.0 collective-permute-done.5.rest_3_
  20.2 2.3 %attention.1.rest_4_ = bf16[8,8,2048]{2,1,0:T(8,128)(2,1)} custom-call(s32[7,9]{1,0:T(8,128)S(1)} %get-tuple-element.22.plan, bf16[256,256]{1,0:T(8,128)(2,1)S(1)} %copy-done.2, bf16[256,256]{1,0:T(8,128)(2,1)S(1)} %copy-done.3, f32[80,128]{1,0:T(8,128)S(1)} %copy-done.1, f32[80,128]{1,0:T(8,128)S(1)} %copy-done, ...), custom_call_target="tpu_custom_call" | custom-call | tf_op jit(solution)/shard_map/attention/pallas_call | solution.py:409
  22.6 0.0 collective-permute-done.6.rest_1_
  22.6 0.0 collective-permute-done.7.rest_2_
  22.6 0.7 %place_pages.1 = bf16[16,2,1024]{2,1,0:T(2,128)(2,1)} custom-call(bf16[32,256]{1,0:T(8,128)(2,1)S(1)} %get-tuple-element.30.rest_0_, bf16[32,256]{1,0:T(8,128)(2,1)S(1)} %collective-permute-done.6.rest_1_, bf16[32,256]{1,0:T(8,128)(2,1)S(1)} %collective-permute-done.7.rest_2_, bf16[32,256]{1,0:T(8,128)(2,1)S(1)} %collective-permute-done.8.rest_3_, ...), custom_call_target="tpu_custom_call" | custom-call | tf_op jit(solution)/shard_map/place_pages/pallas_call | solution.py:419
  (17 shorter events, 0.0 us)
Async XLA Ops:
  1.8 7.0 %collective-permute-start = (bf16[4,8,512]{2,1,0:T(8,128)(2,1)S(1)}, bf16[4,8,512]{2,1,0:T(8,128)(2,1)S(1)}, u32[]{:S(2)}, u32[]{:S(2)}) collective-permute-start(bf16[4,8,512]{2,1,0:T(8,128)(2,1)S(1)} %get-tuple-element.19), channel_id=1, source_target_pairs={{0,4},{4,8},{8,12},{12,0},{1,5},{5,9},{9,13},{13,1},{2,6},{6,10},{... | collective-permute-start | bytes 98312 | tf_op jit(solution)/shard_map/ppermute | solution.py:335
  4.8 5.2 %collective-permute-start.1 = (bf16[4,8,512]{2,1,0:T(8,128)(2,1)S(1)}, bf16[4,8,512]{2,1,0:T(8,128)(2,1)S(1)}, u32[]{:S(2)}, u32[]{:S(2)}) collective-permute-start(bf16[4,8,512]{2,1,0:T(8,128)(2,1)S(1)} %get-tuple-element.20), channel_id=1, source_target_pairs={{0,8},{4,12},{8,0},{12,4},{1,9},{5,13},{9,1},{13,5},{2,10},{6,14},... | collective-permute-start | bytes 98312 | tf_op jit(solution)/shard_map/ppermute | solution.py:335
  7.4 3.9 %collective-permute-start.2 = (bf16[4,8,512]{2,1,0:T(8,128)(2,1)S(1)}, bf16[4,8,512]{2,1,0:T(8,128)(2,1)S(1)}, u32[]{:S(2)}, u32[]{:S(2)}) collective-permute-start(bf16[4,8,512]{2,1,0:T(8,128)(2,1)S(1)} %get-tuple-element.21), channel_id=1, source_target_pairs={{0,12},{4,0},{8,4},{12,8},{1,13},{5,1},{9,5},{13,9},{2,14},{6,2},{... | collective-permute-start | bytes 98312 | tf_op jit(solution)/shard_map/ppermute | solution.py:335
  11.3 4.0 %copy-start = (f32[80,128]{1,0:T(8,128)S(1)}, f32[80,128]{1,0:T(8,128)}, u32[]{:S(2)}) copy-start(f32[80,128]{1,0:T(8,128)} %constant.5.clone.sine) | copy-start | bytes 122884
  11.3 4.0 %copy-start.1 = (f32[80,128]{1,0:T(8,128)S(1)}, f32[80,128]{1,0:T(8,128)}, u32[]{:S(2)}) copy-start(f32[80,128]{1,0:T(8,128)} %constant.4.clone.cosine) | copy-start | bytes 122884
  11.3 4.0 %copy-start.4 = (s32[4,4]{1,0:T(4,128)S(1)}, s32[4,4]{1,0:T(4,128)}, u32[]{:S(2)}) copy-start(s32[4,4]{1,0:T(4,128)} %new_blocks.1) | copy-start | bytes 196
  11.3 4.0 %copy-start.5 = (s32[4,4]{1,0:T(4,128)S(1)}, s32[4,4]{1,0:T(4,128)}, u32[]{:S(2)}) copy-start(s32[4,4]{1,0:T(4,128)} %owner.1) | copy-start | bytes 196
  11.3 4.0 %copy-start.6 = (s32[4,4]{1,0:T(4,128)S(1)}, s32[4,4]{1,0:T(4,128)}, u32[]{:S(2)}) copy-start(s32[4,4]{1,0:T(4,128)} %prefix_len.1) | copy-start | bytes 196
  11.4 4.0 %copy-start.7 = (s32[4,4]{1,0:T(4,128)S(1)}, s32[4,4]{1,0:T(4,128)}, u32[]{:S(2)}) copy-start(s32[4,4]{1,0:T(4,128)} %page_start.1) | copy-start | bytes 196
  11.4 4.0 %copy-start.8 = (s32[4]{0:T(128)S(1)}, s32[4]{0:T(128)}, u32[]{:S(2)}) copy-start(s32[4]{0:T(128)} %spread.1) | copy-start | bytes 52
  11.4 8.9 %copy-start.3 = (bf16[256,256]{1,0:T(8,128)(2,1)S(1)}, bf16[256,256]{1,0:T(8,128)(2,1)}, u32[]{:S(2)}) copy-start(bf16[256,256]{1,0:T(8,128)(2,1)} %prefix_values.1) | copy-start | bytes 393220
  11.4 8.8 %copy-start.2 = (bf16[256,256]{1,0:T(8,128)(2,1)S(1)}, bf16[256,256]{1,0:T(8,128)(2,1)}, u32[]{:S(2)}) copy-start(bf16[256,256]{1,0:T(8,128)(2,1)} %prefix_keys.1) | copy-start | bytes 393220
  11.4 7.4 %collective-permute-start.3 = (bf16[2,8,2560]{2,1,0:T(8,128)(2,1)S(1)}, bf16[2,8,2560]{2,1,0:T(8,128)(2,1)S(1)}, u32[]{:S(2)}, u32[]{:S(2)}) collective-permute-start(bf16[2,8,2560]{2,1,0:T(8,128)(2,1)S(1)} %get-tuple-element.27), channel_id=1, source_target_pairs={{0,4},{4,8},{8,12},{12,0},{1,5},{5,9},{9,13},{13,1},{2,6},{6,10},{... | collective-permute-start | bytes 245768 | tf_op jit(solution)/shard_map/ppermute | solution.py:335
  11.7 8.5 %collective-permute-start.4 = (bf16[2,8,2560]{2,1,0:T(8,128)(2,1)S(1)}, bf16[2,8,2560]{2,1,0:T(8,128)(2,1)S(1)}, u32[]{:S(2)}, u32[]{:S(2)}) collective-permute-start(bf16[2,8,2560]{2,1,0:T(8,128)(2,1)S(1)} %get-tuple-element.28), channel_id=1, source_target_pairs={{0,8},{4,12},{8,0},{12,4},{1,9},{5,13},{9,1},{13,5},{2,10},{6,14},... | collective-permute-start | bytes 245768 | tf_op jit(solution)/shard_map/ppermute | solution.py:335
  15.2 5.0 %collective-permute-start.5 = (bf16[2,8,2560]{2,1,0:T(8,128)(2,1)S(1)}, bf16[2,8,2560]{2,1,0:T(8,128)(2,1)S(1)}, u32[]{:S(2)}, u32[]{:S(2)}) collective-permute-start(bf16[2,8,2560]{2,1,0:T(8,128)(2,1)S(1)} %get-tuple-element.29), channel_id=1, source_target_pairs={{0,12},{4,0},{8,4},{12,8},{1,13},{5,1},{9,5},{13,9},{2,14},{6,2},{... | collective-permute-start | bytes 245768 | tf_op jit(solution)/shard_map/ppermute | solution.py:335
  17.2 5.4 %collective-permute-start.6 = (bf16[32,256]{1,0:T(8,128)(2,1)S(1)}, bf16[32,256]{1,0:T(8,128)(2,1)S(1)}, u32[]{:S(2)}, u32[]{:S(2)}) collective-permute-start(bf16[32,256]{1,0:T(8,128)(2,1)S(1)} %get-tuple-element.31), channel_id=1, source_target_pairs={{0,1},{1,2},{2,3},{3,0},{4,5},{5,6},{6,7},{7,4},{8,9},{9,10},{10,1... | collective-permute-start | bytes 49160 | tf_op jit(solution)/shard_map/ppermute | solution.py:335
  17.2 5.3 %collective-permute-start.7 = (bf16[32,256]{1,0:T(8,128)(2,1)S(1)}, bf16[32,256]{1,0:T(8,128)(2,1)S(1)}, u32[]{:S(2)}, u32[]{:S(2)}) collective-permute-start(bf16[32,256]{1,0:T(8,128)(2,1)S(1)} %get-tuple-element.32), channel_id=1, source_target_pairs={{0,2},{1,3},{2,0},{3,1},{4,6},{5,7},{6,4},{7,5},{8,10},{9,11},{10,... | collective-permute-start | bytes 49160 | tf_op jit(solution)/shard_map/ppermute | solution.py:335
  18.8 3.8 %collective-permute-start.8 = (bf16[32,256]{1,0:T(8,128)(2,1)S(1)}, bf16[32,256]{1,0:T(8,128)(2,1)S(1)}, u32[]{:S(2)}, u32[]{:S(2)}) collective-permute-start(bf16[32,256]{1,0:T(8,128)(2,1)S(1)} %get-tuple-element.33), channel_id=1, source_target_pairs={{0,3},{1,0},{2,1},{3,2},{4,7},{5,4},{6,5},{7,6},{8,11},{9,8},{10,9... | collective-permute-start | bytes 49160 | tf_op jit(solution)/shard_map/ppermute | solution.py:335

commit v2 on v1

--- a/solution.py
+++ b/solution.py
@@ -18,6 +18,7 @@
 
 SMEM = pl.BlockSpec(memory_space=pltpu.SMEM)
 VMEM = pl.BlockSpec(memory_space=pltpu.VMEM)
+JOINED = 1
 PROMPT, OFFSET, LIVE, CACHED, SOURCE, COLUMN, PLACE = range(7)
 ANY = pl.BlockSpec(memory_space=pl.ANY)
 HBM = pl.BlockSpec(memory_space=pltpu.HBM)
@@ -50,7 +51,8 @@
 def dispatch_kernel(
     groups, spread_in, turn_in, new_blocks_in, owner_in, queries_in, keys_in, values_in, *rest
 ):
-    outs, handed, rest = rest[:groups], rest[groups : 2 * groups], rest[2 * groups :]
+    outs, handed, rest = rest[:groups], list(rest[groups : 2 * groups - 1]), rest[2 * groups - 1 :]
+    handed.insert(JOINED, None)
     spread, turn, new_blocks, owner, queries, keys, values, table, sem = rest
     own = lax.axis_index("group")
     slots, _, width_q = queries.shape
@@ -109,16 +111,21 @@
     for distance in range(groups):
         first_slot = column_of(spread, groups, distance) + turn[own]
         out = outs[distance]
+        wide = 2 * width_k
+        per_slot = width_q // wide + 1
         for step in range(capacity):
             source = lax.rem(first_slot + groups * step, slots)
-            out[step, :, :width_q] = queries[source]
-            out[step, :, width_q : width_q + width_k] = keys[source]
-            out[step, :, width_q + width_k :] = values[source]
+            for n in range(per_slot - 1):
+                out[step * per_slot + n] = queries[source, :, n * wide : (n + 1) * wide]
+            last = step * per_slot + per_slot - 1
+            out[last, :, :width_k] = keys[source]
+            out[last, :, width_k:] = values[source]
+        target, base = (out, capacity * per_slot) if distance == JOINED else (handed[distance], 0)
 
         def page(g):
             source = table[distance * groups + g]
-            handed[distance][g, :, :width_k] = keys[source]
-            handed[distance][g, :, width_k:] = values[source]
+            target[base + g, :, :width_k] = keys[source]
+            target[base + g, :, width_k:] = values[source]
 
         loop(groups, page)
 
@@ -197,7 +204,8 @@
     width_k = rows.shape[1]
     tokens = BLOCK // tensors
     for distance in range(groups):
-        blocks[distance * groups : (distance + 1) * groups] = chunks[distance][...]
+        first = chunks[distance].shape[0] - groups
+        blocks[distance * groups : (distance + 1) * groups] = chunks[distance][first:]
     make_plan(groups, own, spread, new_blocks, prefix_len, owner, page_start, plan)
 
     def assemble(page):
@@ -229,6 +237,12 @@
         outs[distance][...] = moved[distance * size : (distance + 1) * size]
 
 
+def columns(chunk, step, width_q, first, width):
+    wide = chunk.shape[2]
+    row = step * (width_q // wide + 1) + first // wide
+    return chunk[row, :, first % wide : first % wide + width]
+
+
 def attention_kernel(groups, heads_q, heads_k, plan, prefix_keys, prefix_values, cosine, sine, *rest):
     arrived, (out, new_keys, new_values) = rest[:groups], rest[groups:]
     slots = out.shape[0]
@@ -248,17 +262,17 @@
         first_slot = plan[COLUMN, distance]
         for step in range(capacity):
             j = first_slot + groups * step
-            here = arrived[distance].at[step]
+            here = functools.partial(columns, arrived[distance], step, width_q)
             cos = cosine[pl.ds(plan[OFFSET, j], BLOCK), :]
             sin = sine[pl.ds(plan[OFFSET, j], BLOCK), :]
             new_keys[j] = jnp.concatenate(
                 [
-                    turned(here[:, first : first + HEAD].astype(jnp.float32), cos, sin)
+                    turned(here(first, HEAD).astype(jnp.float32), cos, sin)
                     for first in range(width_q, width_q + width_k, HEAD)
                 ],
                 axis=1,
             )
-            new_values[j] = here[:, width_q + width_k :].astype(jnp.float32)
+            new_values[j] = here(width_q + width_k, width_k).astype(jnp.float32)
             blocks.append((j, here, cos, sin))
 
     for at in range(0, len(blocks), 8):
@@ -274,7 +288,7 @@
                 key = jnp.concatenate([prefix_keys[region, part], new_key.astype(jnp.bfloat16)], axis=0)
                 query = jnp.concatenate(
                     [
-                        turned(here[:, n * HEAD : (n + 1) * HEAD].astype(jnp.float32), cos, sin)
+                        turned(here(n * HEAD, HEAD).astype(jnp.float32), cos, sin)
                         for n in range(h * ratio, (h + 1) * ratio)
                     ],
                     axis=0,
@@ -332,7 +346,8 @@
 def shifted(chunks, axis):
     size = lax.axis_size(axis)
     return [chunks[0]] + [
-        lax.ppermute(chunks[d], axis, [(i, (i + d) % size) for i in range(size)])
+        chunks[d] is not None
+        and lax.ppermute(chunks[d], axis, [(i, (i + d) % size) for i in range(size)])
         for d in range(1, size)
     ]
 
@@ -367,13 +382,20 @@
     blocks_k = keys.reshape(slots, BLOCK, width_k)
     blocks_v = values.reshape(slots, BLOCK, width_k)
 
-    chunk = jax.ShapeDtypeStruct((capacity, BLOCK, width_q + 2 * width_k), jnp.bfloat16)
-    page_chunk = jax.ShapeDtypeStruct((groups, BLOCK, 2 * width_k), jnp.bfloat16)
+    wide = 2 * width_k
+    chunk_rows = capacity * (width_q // wide + 1)
+
+    def chunk(rows):
+        return jax.ShapeDtypeStruct((rows, BLOCK, wide), jnp.bfloat16)
+
     sent = pl.pallas_call(
         functools.partial(dispatch_kernel, groups),
-        out_shape=[chunk] * groups + [page_chunk] * groups,
+        out_shape=[
+            chunk(chunk_rows + (groups if distance == JOINED else 0)) for distance in range(groups)
+        ]
+        + [chunk(groups)] * (groups - 1),
         in_specs=[HBM] * 7,
-        out_specs=[VMEM] * (2 * groups),
+        out_specs=[VMEM] * (2 * groups - 1),
         scratch_shapes=[
             *(pltpu.SMEM(array.shape, jnp.int32) for array in (spread, turn, new_blocks, owner)),
             *(pltpu.VMEM(array.shape, jnp.bfloat16) for array in (blocks_q, blocks_k, blocks_v)),
@@ -388,8 +410,13 @@
             for operand in (spread, turn, new_blocks, owner, blocks_q, blocks_k, blocks_v)
         )
     )
-    handed = shifted(sent[groups:], "group")
-    arrived = shifted([sent[0], *after(sent[1:groups], handed[1:])], "group")
+    own, pages_only = list(sent[:groups]), list(sent[groups:])
+    pages_only.insert(JOINED, own[JOINED])
+    handed = shifted(pages_only, "group")
+    later = [distance for distance in range(1, groups) if distance != JOINED]
+    held = dict(zip(later, after([own[distance] for distance in later], handed[1:])))
+    moved = shifted([own[0]] + [held.get(distance) for distance in range(1, groups)], "group")
+    arrived = [handed[n] if n == JOINED else moved[n] for n in range(groups)]
 
     part = jax.ShapeDtypeStruct((pages * 2 * tokens, width_k), jnp.bfloat16)
     *finished, plan = pl.pallas_call(

time: 23.4 us -> 23.3 us (level)
  starting transfers between devices: 13.9 us -> 13.5 us
  waiting for transfers between devices: 2.63 us -> 2.89 us
    ppermute x9 -> x8, starting transfers between devices: 13.9 us -> 13.5 us  [shifted(): lax.ppermute(chunks[d], axis, [(i, (i + d) % size) for i in range(size)])]
    ppermute x9 -> x8, waiting for transfers between devices: 2.63 us -> 2.89 us  [shifted(): lax.ppermute(chunks[d], axis, [(i, (i + d) % size) for i in range(size)])]
  transfers between devices with their start and end apart: 9 -> 8, of which waited for: 2 -> 2; matrix products, arithmetic and copies ran while one was open for 0% -> 0% of each run, Pallas kernels for 18% -> 18%
where the time goes in v2:
time: 23.3 us; the launch traced here: 23.2 us
  starting transfers between devices  13.5 us (58%)
  Pallas kernels  5.95 us (26%)
  waiting for transfers between devices  2.89 us (12%)
  between operations  0.76 us (3%)
    ppermute x8, starting transfers between devices, shifted(): lax.ppermute(chunks[d], axis, [(i, (i + d) % size) for i in range(size)])  13.5 us
    ppermute x8, waiting for transfers between devices, shifted(): lax.ppermute(chunks[d], axis, [(i, (i + d) % size) for i in range(size)])  2.89 us
    pallas_call x1, Pallas kernels, per_device(): pl.pallas_call(functools.partial(attention_kernel, groups, heads_q, heads...  2.34 us
    pallas_call x1, Pallas kernels, per_device(): pl.pallas_call(functools.partial(pages_kernel, groups, tensors), out_shap...  1.8 us
    pallas_call x1, Pallas kernels, per_device(): pl.pallas_call(functools.partial(dispatch_kernel, groups), out_shape=[chu...  1.11 us
    pallas_call x1, Pallas kernels, per_device(): pl.pallas_call(functools.partial(cache_kernel, tensors), out_shape=jax.Sh...  0.69 us
  transfers between devices with their start and end apart: 8, of which 2 were waited for; matrix products, arithmetic and copies ran while one was open for 0% of the time, Pallas kernels for 18%

profile of v2, /device:TPU:0, one launch (start us, length us, event | category | flops | bytes accessed | tf_op | source)
XLA Modules:
  0.0 23.2 jit_solution(13674473259944834259)
XLA Ops:
  0.6 1.1 %dispatch.1 = (bf16[10,8,512]{2,1,0:T(8,128)(2,1)S(1)}, bf16[14,8,512]{2,1,0:T(8,128)(2,1)S(1)}, bf16[10,8,512]{2,1,0:T(8,128)(2,1)S(1)}, bf16[10,8,512]{2,1,0:T...) custom-call(s32[4]{0:T(128)} %spread.1, ...), custom_call_target="tpu_custom_call" | custom-call | tf_op jit(solution)/shard_map/dispatch/pallas_call | solution.py:391
  1.8 3.1 %collective-permute-start = (bf16[14,8,512]{2,1,0:T(8,128)(2,1)S(1)}, bf16[14,8,512]{2,1,0:T(8,128)(2,1)S(1)}, u32[]{:S(2)}, u32[]{:S(2)}) collective-permute-start(bf16[14,8,512]{2,1,0:T(8,128)(2,1)S(1)} %get-tuple-element.17), channel_id=1, source_target_pairs={{0,4},{4,8},{8,12},{12,0},{1,5},{5,9},{9,13},{13,1},{2,6},{6,10},{... | collective-permute-start | bytes 344072 | tf_op jit(solution)/shard_map/ppermute | solution.py:350
  4.8 2.6 %collective-permute-start.1 = (bf16[4,8,512]{2,1,0:T(8,128)(2,1)S(1)}, bf16[4,8,512]{2,1,0:T(8,128)(2,1)S(1)}, u32[]{:S(2)}, u32[]{:S(2)}) collective-permute-start(bf16[4,8,512]{2,1,0:T(8,128)(2,1)S(1)} %get-tuple-element.18), channel_id=1, source_target_pairs={{0,8},{4,12},{8,0},{12,4},{1,9},{5,13},{9,1},{13,5},{2,10},{6,14},... | collective-permute-start | bytes 98312 | tf_op jit(solution)/shard_map/ppermute | solution.py:350
  7.4 1.3 %collective-permute-start.2 = (bf16[4,8,512]{2,1,0:T(8,128)(2,1)S(1)}, bf16[4,8,512]{2,1,0:T(8,128)(2,1)S(1)}, u32[]{:S(2)}, u32[]{:S(2)}) collective-permute-start(bf16[4,8,512]{2,1,0:T(8,128)(2,1)S(1)} %get-tuple-element.19), channel_id=1, source_target_pairs={{0,12},{4,0},{8,4},{12,8},{1,13},{5,1},{9,5},{13,9},{2,14},{6,2},{... | collective-permute-start | bytes 98312 | tf_op jit(solution)/shard_map/ppermute | solution.py:350
  8.8 2.7 %collective-permute-done.1.rest_2_.refs_3_ = bf16[4,8,512]{2,1,0:T(8,128)(2,1)S(1)} collective-permute-done((bf16[4,8,512]{2,1,0:T(8,128)(2,1)S(1)}, bf16[4,8,512]{2,1,0:T(8,128)(2,1)S(1)}, u32[]{:S(2)}, u32[]{:S(2)}) %collective-permute-start.1) | collective-permute-done | bytes 32800 | tf_op jit(solution)/shard_map/ppermute | solution.py:350
  11.5 0.1 collective-permute-done.2.rest_3_.refs_4_
  11.6 0.0 collective-permute-done.rest_1_.refs_2_
  11.7 0.0 copy-start.7
  11.7 0.0 copy-start.5
  11.7 0.0 copy-start.4
  11.7 0.8 %collective-permute-start.3 = (bf16[10,8,512]{2,1,0:T(8,128)(2,1)S(1)}, bf16[10,8,512]{2,1,0:T(8,128)(2,1)S(1)}, u32[]{:S(2)}, u32[]{:S(2)}) collective-permute-start(bf16[10,8,512]{2,1,0:T(8,128)(2,1)S(1)} %get-tuple-element.24), channel_id=1, source_target_pairs={{0,8},{4,12},{8,0},{12,4},{1,9},{5,13},{9,1},{13,5},{2,10},{6,14},... | collective-permute-start | bytes 245768 | tf_op jit(solution)/shard_map/ppermute | solution.py:350
  12.5 2.7 %collective-permute-start.4 = (bf16[10,8,512]{2,1,0:T(8,128)(2,1)S(1)}, bf16[10,8,512]{2,1,0:T(8,128)(2,1)S(1)}, u32[]{:S(2)}, u32[]{:S(2)}) collective-permute-start(bf16[10,8,512]{2,1,0:T(8,128)(2,1)S(1)} %get-tuple-element.25), channel_id=1, source_target_pairs={{0,12},{4,0},{8,4},{12,8},{1,13},{5,1},{9,5},{13,9},{2,14},{6,2},{... | collective-permute-start | bytes 245768 | tf_op jit(solution)/shard_map/ppermute | solution.py:350
  15.2 0.0 copy-start.2
  15.2 0.0 copy-start.3
  15.2 1.8 %finish_pages.1 = (bf16[32,256]{1,0:T(8,128)(2,1)S(1)}, bf16[32,256]{1,0:T(8,128)(2,1)S(1)}, bf16[32,256]{1,0:T(8,128)(2,1)S(1)}, bf16[32,256]{1,0:T(8,128)(2,1)S(1)}, s32[7,9]{1,0:T(8,128)S(1)}) custom-call(s32[4]{0:T(128)S(1)} %copy-done.8, s32[4,4]{1,0:T(4,128)S(1)} %copy-done.4, s32[4,4]{1,0:T(4,128)S(1)} %copy-done.6, s32[4,4]{1,0:T(4,128)S(1)} %copy-done.5, ...), custom_call_target="tpu_custom_call" | custom-call | tf_op jit(solution)/shard_map/finish_pages/pallas_call | solution.py:422
  17.0 0.1 collective-permute-start.5
  17.1 1.6 %collective-permute-start.6 = (bf16[32,256]{1,0:T(8,128)(2,1)S(1)}, bf16[32,256]{1,0:T(8,128)(2,1)S(1)}, u32[]{:S(2)}, u32[]{:S(2)}) collective-permute-start(bf16[32,256]{1,0:T(8,128)(2,1)S(1)} %get-tuple-element.28), channel_id=1, source_target_pairs={{0,2},{1,3},{2,0},{3,1},{4,6},{5,7},{6,4},{7,5},{8,10},{9,11},{10,... | collective-permute-start | bytes 49160 | tf_op jit(solution)/shard_map/ppermute | solution.py:350
  18.7 1.4 %collective-permute-start.7 = (bf16[32,256]{1,0:T(8,128)(2,1)S(1)}, bf16[32,256]{1,0:T(8,128)(2,1)S(1)}, u32[]{:S(2)}, u32[]{:S(2)}) collective-permute-start(bf16[32,256]{1,0:T(8,128)(2,1)S(1)} %get-tuple-element.29), channel_id=1, source_target_pairs={{0,3},{1,0},{2,1},{3,2},{4,7},{5,4},{6,5},{7,6},{8,11},{9,8},{10,9... | collective-permute-start | bytes 49160 | tf_op jit(solution)/shard_map/ppermute | solution.py:350
  20.1 0.0 collective-permute-done.3.rest_2_
  20.1 0.0 collective-permute-done.4.rest_3_
  20.1 2.3 %attention.1.rest_4_ = bf16[8,8,2048]{2,1,0:T(8,128)(2,1)} custom-call(s32[7,9]{1,0:T(8,128)S(1)} %get-tuple-element.20.plan, bf16[256,256]{1,0:T(8,128)(2,1)S(1)} %copy-done.2, bf16[256,256]{1,0:T(8,128)(2,1)S(1)} %copy-done.3, f32[80,128]{1,0:T(8,128)S(1)} %copy-done.1, f32[80,128]{1,0:T(8,128)S(1)} %copy-done, ...), custom_call_target="tpu_custom_call" | custom-call | tf_op jit(solution)/shard_map/attention/pallas_call | solution.py:436
  22.5 0.0 collective-permute-done.6.rest_2_
  22.5 0.0 collective-permute-done.7.rest_3_
  22.5 0.7 %place_pages.1 = bf16[16,2,1024]{2,1,0:T(2,128)(2,1)} custom-call(bf16[32,256]{1,0:T(8,128)(2,1)S(1)} %get-tuple-element.26.rest_0_, bf16[32,256]{1,0:T(8,128)(2,1)S(1)} %collective-permute-done.5.rest_1_, bf16[32,256]{1,0:T(8,128)(2,1)S(1)} %collective-permute-done.6.rest_2_, bf16[32,256]{1,0:T(8,128)(2,1)S(1)} %collective-permute-done.7.rest_3_, ...), custom_call_target="tpu_custom_call" | custom-call | tf_op jit(solution)/shard_map/place_pages/pallas_call | solution.py:446
  (15 shorter events, 0.0 us)
Async XLA Ops:
  1.8 9.9 %collective-permute-start = (bf16[14,8,512]{2,1,0:T(8,128)(2,1)S(1)}, bf16[14,8,512]{2,1,0:T(8,128)(2,1)S(1)}, u32[]{:S(2)}, u32[]{:S(2)}) collective-permute-start(bf16[14,8,512]{2,1,0:T(8,128)(2,1)S(1)} %get-tuple-element.17), channel_id=1, source_target_pairs={{0,4},{4,8},{8,12},{12,0},{1,5},{5,9},{9,13},{13,1},{2,6},{6,10},{... | collective-permute-start | bytes 344072 | tf_op jit(solution)/shard_map/ppermute | solution.py:350
  4.8 6.7 %collective-permute-start.1 = (bf16[4,8,512]{2,1,0:T(8,128)(2,1)S(1)}, bf16[4,8,512]{2,1,0:T(8,128)(2,1)S(1)}, u32[]{:S(2)}, u32[]{:S(2)}) collective-permute-start(bf16[4,8,512]{2,1,0:T(8,128)(2,1)S(1)} %get-tuple-element.18), channel_id=1, source_target_pairs={{0,8},{4,12},{8,0},{12,4},{1,9},{5,13},{9,1},{13,5},{2,10},{6,14},... | collective-permute-start | bytes 98312 | tf_op jit(solution)/shard_map/ppermute | solution.py:350
  7.4 4.2 %collective-permute-start.2 = (bf16[4,8,512]{2,1,0:T(8,128)(2,1)S(1)}, bf16[4,8,512]{2,1,0:T(8,128)(2,1)S(1)}, u32[]{:S(2)}, u32[]{:S(2)}) collective-permute-start(bf16[4,8,512]{2,1,0:T(8,128)(2,1)S(1)} %get-tuple-element.19), channel_id=1, source_target_pairs={{0,12},{4,0},{8,4},{12,8},{1,13},{5,1},{9,5},{13,9},{2,14},{6,2},{... | collective-permute-start | bytes 98312 | tf_op jit(solution)/shard_map/ppermute | solution.py:350
  11.6 3.5 %copy-start = (f32[80,128]{1,0:T(8,128)S(1)}, f32[80,128]{1,0:T(8,128)}, u32[]{:S(2)}) copy-start(f32[80,128]{1,0:T(8,128)} %constant.5.clone.sine) | copy-start | bytes 122884
  11.6 3.5 %copy-start.1 = (f32[80,128]{1,0:T(8,128)S(1)}, f32[80,128]{1,0:T(8,128)}, u32[]{:S(2)}) copy-start(f32[80,128]{1,0:T(8,128)} %constant.4.clone.cosine) | copy-start | bytes 122884
  11.6 3.5 %copy-start.6 = (s32[4,4]{1,0:T(4,128)S(1)}, s32[4,4]{1,0:T(4,128)}, u32[]{:S(2)}) copy-start(s32[4,4]{1,0:T(4,128)} %prefix_len.1) | copy-start | bytes 196
  11.7 3.5 %copy-start.7 = (s32[4,4]{1,0:T(4,128)S(1)}, s32[4,4]{1,0:T(4,128)}, u32[]{:S(2)}) copy-start(s32[4,4]{1,0:T(4,128)} %page_start.1) | copy-start | bytes 196
  11.7 3.5 %copy-start.5 = (s32[4,4]{1,0:T(4,128)S(1)}, s32[4,4]{1,0:T(4,128)}, u32[]{:S(2)}) copy-start(s32[4,4]{1,0:T(4,128)} %owner.1) | copy-start | bytes 196
  11.7 3.5 %copy-start.4 = (s32[4,4]{1,0:T(4,128)S(1)}, s32[4,4]{1,0:T(4,128)}, u32[]{:S(2)}) copy-start(s32[4,4]{1,0:T(4,128)} %new_blocks.1) | copy-start | bytes 196
  11.7 8.4 %collective-permute-start.3 = (bf16[10,8,512]{2,1,0:T(8,128)(2,1)S(1)}, bf16[10,8,512]{2,1,0:T(8,128)(2,1)S(1)}, u32[]{:S(2)}, u32[]{:S(2)}) collective-permute-start(bf16[10,8,512]{2,1,0:T(8,128)(2,1)S(1)} %get-tuple-element.24), channel_id=1, source_target_pairs={{0,8},{4,12},{8,0},{12,4},{1,9},{5,13},{9,1},{13,5},{2,10},{6,14},... | collective-permute-start | bytes 245768 | tf_op jit(solution)/shard_map/ppermute | solution.py:350
  12.5 2.7 %copy-start.8 = (s32[4]{0:T(128)S(1)}, s32[4]{0:T(128)}, u32[]{:S(2)}) copy-start(s32[4]{0:T(128)} %spread.1) | copy-start | bytes 52
  12.5 7.6 %collective-permute-start.4 = (bf16[10,8,512]{2,1,0:T(8,128)(2,1)S(1)}, bf16[10,8,512]{2,1,0:T(8,128)(2,1)S(1)}, u32[]{:S(2)}, u32[]{:S(2)}) collective-permute-start(bf16[10,8,512]{2,1,0:T(8,128)(2,1)S(1)} %get-tuple-element.25), channel_id=1, source_target_pairs={{0,12},{4,0},{8,4},{12,8},{1,13},{5,1},{9,5},{13,9},{2,14},{6,2},{... | collective-permute-start | bytes 245768 | tf_op jit(solution)/shard_map/ppermute | solution.py:350
  15.2 4.9 %copy-start.2 = (bf16[256,256]{1,0:T(8,128)(2,1)S(1)}, bf16[256,256]{1,0:T(8,128)(2,1)}, u32[]{:S(2)}) copy-start(bf16[256,256]{1,0:T(8,128)(2,1)} %prefix_keys.1) | copy-start | bytes 393220
  15.2 4.9 %copy-start.3 = (bf16[256,256]{1,0:T(8,128)(2,1)S(1)}, bf16[256,256]{1,0:T(8,128)(2,1)}, u32[]{:S(2)}) copy-start(bf16[256,256]{1,0:T(8,128)(2,1)} %prefix_values.1) | copy-start | bytes 393220
  17.0 5.4 %collective-permute-start.5 = (bf16[32,256]{1,0:T(8,128)(2,1)S(1)}, bf16[32,256]{1,0:T(8,128)(2,1)S(1)}, u32[]{:S(2)}, u32[]{:S(2)}) collective-permute-start(bf16[32,256]{1,0:T(8,128)(2,1)S(1)} %get-tuple-element.27), channel_id=1, source_target_pairs={{0,1},{1,2},{2,3},{3,0},{4,5},{5,6},{6,7},{7,4},{8,9},{9,10},{10,1... | collective-permute-start | bytes 49160 | tf_op jit(solution)/shard_map/ppermute | solution.py:350
  17.1 5.4 %collective-permute-start.6 = (bf16[32,256]{1,0:T(8,128)(2,1)S(1)}, bf16[32,256]{1,0:T(8,128)(2,1)S(1)}, u32[]{:S(2)}, u32[]{:S(2)}) collective-permute-start(bf16[32,256]{1,0:T(8,128)(2,1)S(1)} %get-tuple-element.28), channel_id=1, source_target_pairs={{0,2},{1,3},{2,0},{3,1},{4,6},{5,7},{6,4},{7,5},{8,10},{9,11},{10,... | collective-permute-start | bytes 49160 | tf_op jit(solution)/shard_map/ppermute | solution.py:350
  18.7 3.8 %collective-permute-start.7 = (bf16[32,256]{1,0:T(8,128)(2,1)S(1)}, bf16[32,256]{1,0:T(8,128)(2,1)S(1)}, u32[]{:S(2)}, u32[]{:S(2)}) collective-permute-start(bf16[32,256]{1,0:T(8,128)(2,1)S(1)} %get-tuple-element.29), channel_id=1, source_target_pairs={{0,3},{1,0},{2,1},{3,2},{4,7},{5,4},{6,5},{7,6},{8,11},{9,8},{10,9... | collective-permute-start | bytes 49160 | tf_op jit(solution)/shard_map/ppermute | solution.py:350

commit v3 on v2

--- a/solution.py
+++ b/solution.py
@@ -193,20 +193,30 @@
         plan[COLUMN, distance] = column_of(spread, groups, distance)
 
 
-def pages_kernel(
-    groups, tensors, spread, new_blocks, prefix_len, owner, page_start, cosine, sine, *rest
-):
-    chunks, rest = rest[:groups], rest[groups:]
-    outs, (plan, blocks, rows) = rest[:tensors], rest[tensors:]
+def plan_kernel(groups, tensors, spread, new_blocks, prefix_len, owner, page_start, _, plan, pick):
     own = lax.axis_index("group")
     own_tensor = lax.axis_index("tensor")
+    make_plan(groups, own, spread, new_blocks, prefix_len, owner, page_start, plan)
     pages = new_blocks.shape[1] * MAXP
+    tokens = BLOCK // tensors
+    size = pages * 2 * tokens
+    row = lax.broadcasted_iota(jnp.int32, pick.shape, 0)
+    col = lax.broadcasted_iota(jnp.int32, pick.shape, 1)
+    share = lax.rem(row // size + own_tensor, tensors)
+    kind, page = (row // tokens) % 2, (row // (2 * tokens)) % pages
+    wanted = (kind * pages + page) * BLOCK + share * tokens + row % tokens
+    pick[...] = (col == wanted).astype(jnp.float32).astype(jnp.bfloat16)
+
+
+def pages_kernel(groups, tensors, plan, pick, cosine, sine, *rest):
+    chunks, rest = rest[:groups], rest[groups:]
+    outs, (blocks, rows) = rest[:tensors], rest[tensors:]
     width_k = rows.shape[1]
-    tokens = BLOCK // tensors
+    pages = rows.shape[0] // (2 * BLOCK)
+    size = pick.shape[0] // tensors
     for distance in range(groups):
         first = chunks[distance].shape[0] - groups
         blocks[distance * groups : (distance + 1) * groups] = chunks[distance][first:]
-    make_plan(groups, own, spread, new_blocks, prefix_len, owner, page_start, plan)
 
     def assemble(page):
         source = plan[SOURCE, page]
@@ -223,15 +233,7 @@
         rows[pl.ds(pl.multiple_of((pages + page) * BLOCK, BLOCK), BLOCK), :] = block[:, width_k:]
 
     loop(pages, assemble)
-    size = pages * 2 * tokens
-    shape = (tensors * size, 2 * pages * BLOCK)
-    row = lax.broadcasted_iota(jnp.int32, shape, 0)
-    col = lax.broadcasted_iota(jnp.int32, shape, 1)
-    share = lax.rem(row // size + own_tensor, tensors)
-    kind, page = (row // tokens) % 2, (row // (2 * tokens)) % pages
-    wanted = (kind * pages + page) * BLOCK + share * tokens + row % tokens
-    pick = (col == wanted).astype(jnp.float32).astype(jnp.bfloat16)
-    moved = jnp.dot(pick, rows[...].astype(jnp.bfloat16), preferred_element_type=jnp.float32)
+    moved = jnp.dot(pick[...], rows[...].astype(jnp.bfloat16), preferred_element_type=jnp.float32)
     moved = moved.astype(jnp.bfloat16)
     for distance in range(tensors):
         outs[distance][...] = moved[distance * size : (distance + 1) * size]
@@ -410,27 +412,39 @@
             for operand in (spread, turn, new_blocks, owner, blocks_q, blocks_k, blocks_v)
         )
     )
+    part_rows = pages * 2 * tokens
+    plan, pick = pl.pallas_call(
+        functools.partial(plan_kernel, groups, tensors),
+        out_shape=[
+            jax.ShapeDtypeStruct((7, max(slots, groups) + 1), jnp.int32),
+            jax.ShapeDtypeStruct((tensors * part_rows, 2 * pages * BLOCK), jnp.bfloat16),
+        ],
+        in_specs=[SMEM] * 5 + [ANY],
+        out_specs=[SMEM, VMEM],
+        compiler_params=params,
+        name="plan",
+    )(spread, new_blocks, prefix_len, owner, page_start, sent[0])
     own, pages_only = list(sent[:groups]), list(sent[groups:])
     pages_only.insert(JOINED, own[JOINED])
     handed = shifted(pages_only, "group")
     later = [distance for distance in range(1, groups) if distance != JOINED]
-    held = dict(zip(later, after([own[distance] for distance in later], handed[1:])))
+    held = dict(zip(later, after([own[distance] for distance in later], [*handed[1:], plan])))
     moved = shifted([own[0]] + [held.get(distance) for distance in range(1, groups)], "group")
     arrived = [handed[n] if n == JOINED else moved[n] for n in range(groups)]
 
-    part = jax.ShapeDtypeStruct((pages * 2 * tokens, width_k), jnp.bfloat16)
-    *finished, plan = pl.pallas_call(
+    part = jax.ShapeDtypeStruct((part_rows, width_k), jnp.bfloat16)
+    finished = pl.pallas_call(
         functools.partial(pages_kernel, groups, tensors),
-        out_shape=[part] * tensors + [jax.ShapeDtypeStruct((7, max(slots, groups) + 1), jnp.int32)],
-        in_specs=[SMEM] * 5 + [VMEM] * (2 + groups),
-        out_specs=[VMEM] * tensors + [SMEM],
+        out_shape=[part] * tensors,
+        in_specs=[SMEM] + [VMEM] * (3 + groups),
+        out_specs=[VMEM] * tensors,
         compiler_params=params,
         scratch_shapes=[
             pltpu.VMEM((groups * groups, BLOCK, 2 * width_k), jnp.bfloat16),
             pltpu.VMEM((2 * pages * BLOCK, width_k), jnp.float32),
         ],
         name="finish_pages",
-    )(spread, new_blocks, prefix_len, owner, page_start, cosine, sine, *handed)
+    )(plan, pick, cosine, sine, *handed)
     parts = shifted(finished, "tensor")
 
     attention = pl.pallas_call(

time: 23.3 us -> 22.5 us (0.966)
  waiting for transfers between devices: 2.89 us -> 1.44 us
  Pallas kernels: 5.95 us -> 6.69 us
    pallas_call x0 -> x1, Pallas kernels: none -> 1.72 us  [per_device(): pl.pallas_call(functools.partial(plan_kernel, groups, tensors), out_shape...]
    ppermute x8, waiting for transfers between devices: 2.89 us -> 1.44 us  [shifted(): lax.ppermute(chunks[d], axis, [(i, (i + d) % size) for i in range(size)])]
    pallas_call x1, Pallas kernels: 1.8 us -> 0.83 us  [per_device(): pl.pallas_call(functools.partial(pages_kernel, groups, tensors), out_shap...]
  transfers between devices with their start and end apart: 8 -> 8, of which waited for: 2 -> 3; matrix products, arithmetic and copies ran while one was open for 0% -> 0% of each run, Pallas kernels for 18% -> 22%
where the time goes in v3:
time: 22.5 us; the launch traced here: 22.4 us
  starting transfers between devices  13.5 us (60%)
  Pallas kernels  6.69 us (30%)
  waiting for transfers between devices  1.44 us (6%)
  between operations  0.72 us (3%)
    ppermute x8, starting transfers between devices, shifted(): lax.ppermute(chunks[d], axis, [(i, (i + d) % size) for i in range(size)])  13.5 us
    pallas_call x1, Pallas kernels, per_device(): pl.pallas_call(functools.partial(attention_kernel, groups, heads_q, heads...  2.33 us
    pallas_call x1, Pallas kernels, per_device(): pl.pallas_call(functools.partial(plan_kernel, groups, tensors), out_shape...  1.72 us
    ppermute x8, waiting for transfers between devices, shifted(): lax.ppermute(chunks[d], axis, [(i, (i + d) % size) for i in range(size)])  1.44 us
    pallas_call x1, Pallas kernels, per_device(): pl.pallas_call(functools.partial(dispatch_kernel, groups), out_shape=[chu...  1.11 us
    pallas_call x1, Pallas kernels, per_device(): pl.pallas_call(functools.partial(pages_kernel, groups, tensors), out_shap...  0.83 us
    pallas_call x1, Pallas kernels, per_device(): pl.pallas_call(functools.partial(cache_kernel, tensors), out_shape=jax.Sh...  0.69 us
  transfers between devices with their start and end apart: 8, of which 3 were waited for; matrix products, arithmetic and copies ran while one was open for 0% of the time, Pallas kernels for 22%

profile of v3, /device:TPU:0, one launch (start us, length us, event | category | flops | bytes accessed | tf_op | source)
XLA Modules:
  0.0 22.4 jit_solution(17713741132143897321)
XLA Ops:
  0.6 1.1 %dispatch.1 = (bf16[10,8,512]{2,1,0:T(8,128)(2,1)S(1)}, bf16[14,8,512]{2,1,0:T(8,128)(2,1)S(1)}, bf16[10,8,512]{2,1,0:T(8,128)(2,1)S(1)}, bf16[10,8,512]{2,1,0:T...) custom-call(s32[4]{0:T(128)} %spread.1, ...), custom_call_target="tpu_custom_call" | custom-call | tf_op jit(solution)/shard_map/dispatch/pallas_call | solution.py:393
  1.8 0.0 copy-start.7
  1.8 3.1 %collective-permute-start = (bf16[14,8,512]{2,1,0:T(8,128)(2,1)S(1)}, bf16[14,8,512]{2,1,0:T(8,128)(2,1)S(1)}, u32[]{:S(2)}, u32[]{:S(2)}) collective-permute-start(bf16[14,8,512]{2,1,0:T(8,128)(2,1)S(1)} %get-tuple-element.19), channel_id=1, source_target_pairs={{0,4},{4,8},{8,12},{12,0},{1,5},{5,9},{9,13},{13,1},{2,6},{6,10},{... | collective-permute-start | bytes 344072 | tf_op jit(solution)/shard_map/ppermute | solution.py:352
  4.9 2.6 %collective-permute-start.1 = (bf16[4,8,512]{2,1,0:T(8,128)(2,1)S(1)}, bf16[4,8,512]{2,1,0:T(8,128)(2,1)S(1)}, u32[]{:S(2)}, u32[]{:S(2)}) collective-permute-start(bf16[4,8,512]{2,1,0:T(8,128)(2,1)S(1)} %get-tuple-element.22), channel_id=1, source_target_pairs={{0,8},{4,12},{8,0},{12,4},{1,9},{5,13},{9,1},{13,5},{2,10},{6,14},... | collective-permute-start | bytes 98312 | tf_op jit(solution)/shard_map/ppermute | solution.py:352
  7.4 1.3 %collective-permute-start.2 = (bf16[4,8,512]{2,1,0:T(8,128)(2,1)S(1)}, bf16[4,8,512]{2,1,0:T(8,128)(2,1)S(1)}, u32[]{:S(2)}, u32[]{:S(2)}) collective-permute-start(bf16[4,8,512]{2,1,0:T(8,128)(2,1)S(1)} %get-tuple-element.23), channel_id=1, source_target_pairs={{0,12},{4,0},{8,4},{12,8},{1,13},{5,1},{9,5},{13,9},{2,14},{6,2},{... | collective-permute-start | bytes 98312 | tf_op jit(solution)/shard_map/ppermute | solution.py:352
  8.8 1.7 %plan.1 = (s32[7,9]{1,0:T(8,128)S(1)}, bf16[128,128]{1,0:T(8,128)(2,1)S(1)}) custom-call(s32[4]{0:T(128)S(1)} %copy-done.6, s32[4,4]{1,0:T(4,128)S(1)} %copy-done.4, s32[4,4]{1,0:T(4,128)S(1)} %copy-done.7, s32[4,4]{1,0:T(4,128)S(1)} %copy-done.5, s32[4,4]{1,0:T(4,128)S(1)} %copy-done.8, bf16[10,8,512]{2,1,0:T(8,128)(2,1)S(1)} %get-tuple-element.17._.rest_0_), custom_call_target="tpu_custom_call" | custom-call | tf_op jit(solution)/shard_map/plan/pallas_call | solution.py:416
  10.5 1.0 %collective-permute-done.1.refs_3_.rest_2_ = bf16[4,8,512]{2,1,0:T(8,128)(2,1)S(1)} collective-permute-done((bf16[4,8,512]{2,1,0:T(8,128)(2,1)S(1)}, bf16[4,8,512]{2,1,0:T(8,128)(2,1)S(1)}, u32[]{:S(2)}, u32[]{:S(2)}) %collective-permute-start.1) | collective-permute-done | bytes 32800 | tf_op jit(solution)/shard_map/ppermute | solution.py:352
  11.5 0.1 collective-permute-done.2.refs_4_.rest_3_
  11.7 0.0 collective-permute-done.refs_2_.rest_1_
  11.7 0.8 %collective-permute-start.3 = (bf16[10,8,512]{2,1,0:T(8,128)(2,1)S(1)}, bf16[10,8,512]{2,1,0:T(8,128)(2,1)S(1)}, u32[]{:S(2)}, u32[]{:S(2)}) collective-permute-start(bf16[10,8,512]{2,1,0:T(8,128)(2,1)S(1)} %get-tuple-element.24), channel_id=1, source_target_pairs={{0,8},{4,12},{8,0},{12,4},{1,9},{5,13},{9,1},{13,5},{2,10},{6,14},... | collective-permute-start | bytes 245768 | tf_op jit(solution)/shard_map/ppermute | solution.py:352
  12.5 2.7 %collective-permute-start.4 = (bf16[10,8,512]{2,1,0:T(8,128)(2,1)S(1)}, bf16[10,8,512]{2,1,0:T(8,128)(2,1)S(1)}, u32[]{:S(2)}, u32[]{:S(2)}) collective-permute-start(bf16[10,8,512]{2,1,0:T(8,128)(2,1)S(1)} %get-tuple-element.25), channel_id=1, source_target_pairs={{0,12},{4,0},{8,4},{12,8},{1,13},{5,1},{9,5},{13,9},{2,14},{6,2},{... | collective-permute-start | bytes 245768 | tf_op jit(solution)/shard_map/ppermute | solution.py:352
  15.1 0.0 copy-done.1
  15.1 0.8 %finish_pages.1 = (bf16[32,256]{1,0:T(8,128)(2,1)S(1)}, bf16[32,256]{1,0:T(8,128)(2,1)S(1)}, bf16[32,256]{1,0:T(8,128)(2,1)S(1)}, bf16[32,256]{1,0:T(8,128)(2,1)S(1)}) custom-call(s32[7,9]{1,0:T(8,128)S(1)} %get-tuple-element.18.refs_5_.plan, bf16[128,128]{1,0:T(8,128)(2,1)S(1)} %get-tuple-element.26.pick, f32[80,128]{1,0:T(8,128)S(1)} %copy-done.1, ...), custom_call_target="tpu_custom_call" | custom-call | tf_op jit(solution)/shard_map/finish_pages/pallas_call | solution.py:436
  16.0 0.1 collective-permute-start.5
  16.1 1.6 %collective-permute-start.6 = (bf16[32,256]{1,0:T(8,128)(2,1)S(1)}, bf16[32,256]{1,0:T(8,128)(2,1)S(1)}, u32[]{:S(2)}, u32[]{:S(2)}) collective-permute-start(bf16[32,256]{1,0:T(8,128)(2,1)S(1)} %get-tuple-element.30), channel_id=1, source_target_pairs={{0,2},{1,3},{2,0},{3,1},{4,6},{5,7},{6,4},{7,5},{8,10},{9,11},{10,... | collective-permute-start | bytes 49160 | tf_op jit(solution)/shard_map/ppermute | solution.py:352
  17.7 1.4 %collective-permute-start.7 = (bf16[32,256]{1,0:T(8,128)(2,1)S(1)}, bf16[32,256]{1,0:T(8,128)(2,1)S(1)}, u32[]{:S(2)}, u32[]{:S(2)}) collective-permute-start(bf16[32,256]{1,0:T(8,128)(2,1)S(1)} %get-tuple-element.31), channel_id=1, source_target_pairs={{0,3},{1,0},{2,1},{3,2},{4,7},{5,4},{6,5},{7,6},{8,11},{9,8},{10,9... | collective-permute-start | bytes 49160 | tf_op jit(solution)/shard_map/ppermute | solution.py:352
  19.0 0.3 %collective-permute-done.3.rest_2_ = bf16[10,8,512]{2,1,0:T(8,128)(2,1)S(1)} collective-permute-done((bf16[10,8,512]{2,1,0:T(8,128)(2,1)S(1)}, bf16[10,8,512]{2,1,0:T(8,128)(2,1)S(1)}, u32[]{:S(2)}, u32[]{:S(2)}) %collective-permute-start.3) | collective-permute-done | bytes 81952 | tf_op jit(solution)/shard_map/ppermute | solution.py:352
  19.3 0.0 collective-permute-done.4.rest_3_
  19.4 0.0 copy-done.3
  19.4 2.3 %attention.1.rest_4_ = bf16[8,8,2048]{2,1,0:T(8,128)(2,1)} custom-call(s32[7,9]{1,0:T(8,128)S(1)} %get-tuple-element.18.refs_5_.plan, bf16[256,256]{1,0:T(8,128)(2,1)S(1)} %copy-done.2, bf16[256,256]{1,0:T(8,128)(2,1)S(1)} %copy-done.3, f32[80,128]{1,0:T(8,128)S(1)} %copy-done.1, f32[80,128]{1,0:T(8,128)S(1)} %copy-done, ...), custom_call_target="tpu_custom_call" | custom-call | tf_op jit(solution)/shard_map/attention/pallas_call | solution.py:450
  21.7 0.0 collective-permute-done.5.rest_1_
  21.7 0.0 collective-permute-done.6.rest_2_
  21.7 0.0 collective-permute-done.7.rest_3_
  21.7 0.7 %place_pages.1 = bf16[16,2,1024]{2,1,0:T(2,128)(2,1)} custom-call(bf16[32,256]{1,0:T(8,128)(2,1)S(1)} %get-tuple-element.28.rest_0_, bf16[32,256]{1,0:T(8,128)(2,1)S(1)} %collective-permute-done.5.rest_1_, bf16[32,256]{1,0:T(8,128)(2,1)S(1)} %collective-permute-done.6.rest_2_, bf16[32,256]{1,0:T(8,128)(2,1)S(1)} %collective-permute-done.7.rest_3_, ...), custom_call_target="tpu_custom_call" | custom-call | tf_op jit(solution)/shard_map/place_pages/pallas_call | solution.py:460
  (16 shorter events, 0.0 us)
Async XLA Ops:
  0.6 8.2 %copy-start.8 = (s32[4,4]{1,0:T(4,128)S(1)}, s32[4,4]{1,0:T(4,128)}, u32[]{:S(2)}) copy-start(s32[4,4]{1,0:T(4,128)} %page_start.1) | copy-start | bytes 196
  1.8 7.0 %copy-start.7 = (s32[4,4]{1,0:T(4,128)S(1)}, s32[4,4]{1,0:T(4,128)}, u32[]{:S(2)}) copy-start(s32[4,4]{1,0:T(4,128)} %prefix_len.1) | copy-start | bytes 196
  1.8 9.9 %collective-permute-start = (bf16[14,8,512]{2,1,0:T(8,128)(2,1)S(1)}, bf16[14,8,512]{2,1,0:T(8,128)(2,1)S(1)}, u32[]{:S(2)}, u32[]{:S(2)}) collective-permute-start(bf16[14,8,512]{2,1,0:T(8,128)(2,1)S(1)} %get-tuple-element.19), channel_id=1, source_target_pairs={{0,4},{4,8},{8,12},{12,0},{1,5},{5,9},{9,13},{13,1},{2,6},{6,10},{... | collective-permute-start | bytes 344072 | tf_op jit(solution)/shard_map/ppermute | solution.py:352
  4.9 4.0 %copy-start.5 = (s32[4,4]{1,0:T(4,128)S(1)}, s32[4,4]{1,0:T(4,128)}, u32[]{:S(2)}) copy-start(s32[4,4]{1,0:T(4,128)} %owner.1) | copy-start | bytes 196
  4.9 4.0 %copy-start.4 = (s32[4,4]{1,0:T(4,128)S(1)}, s32[4,4]{1,0:T(4,128)}, u32[]{:S(2)}) copy-start(s32[4,4]{1,0:T(4,128)} %new_blocks.1) | copy-start | bytes 196
  4.9 6.7 %collective-permute-start.1 = (bf16[4,8,512]{2,1,0:T(8,128)(2,1)S(1)}, bf16[4,8,512]{2,1,0:T(8,128)(2,1)S(1)}, u32[]{:S(2)}, u32[]{:S(2)}) collective-permute-start(bf16[4,8,512]{2,1,0:T(8,128)(2,1)S(1)} %get-tuple-element.22), channel_id=1, source_target_pairs={{0,8},{4,12},{8,0},{12,4},{1,9},{5,13},{9,1},{13,5},{2,10},{6,14},... | collective-permute-start | bytes 98312 | tf_op jit(solution)/shard_map/ppermute | solution.py:352
  7.4 1.4 %copy-start.6 = (s32[4]{0:T(128)S(1)}, s32[4]{0:T(128)}, u32[]{:S(2)}) copy-start(s32[4]{0:T(128)} %spread.1) | copy-start | bytes 52
  7.4 4.2 %collective-permute-start.2 = (bf16[4,8,512]{2,1,0:T(8,128)(2,1)S(1)}, bf16[4,8,512]{2,1,0:T(8,128)(2,1)S(1)}, u32[]{:S(2)}, u32[]{:S(2)}) collective-permute-start(bf16[4,8,512]{2,1,0:T(8,128)(2,1)S(1)} %get-tuple-element.23), channel_id=1, source_target_pairs={{0,12},{4,0},{8,4},{12,8},{1,13},{5,1},{9,5},{13,9},{2,14},{6,2},{... | collective-permute-start | bytes 98312 | tf_op jit(solution)/shard_map/ppermute | solution.py:352
  11.7 3.5 %copy-start = (f32[80,128]{1,0:T(8,128)S(1)}, f32[80,128]{1,0:T(8,128)}, u32[]{:S(2)}) copy-start(f32[80,128]{1,0:T(8,128)} %constant.5.clone.sine) | copy-start | bytes 122884
  11.7 3.5 %copy-start.1 = (f32[80,128]{1,0:T(8,128)S(1)}, f32[80,128]{1,0:T(8,128)}, u32[]{:S(2)}) copy-start(f32[80,128]{1,0:T(8,128)} %constant.4.clone.cosine) | copy-start | bytes 122884
  11.7 7.7 %collective-permute-start.3 = (bf16[10,8,512]{2,1,0:T(8,128)(2,1)S(1)}, bf16[10,8,512]{2,1,0:T(8,128)(2,1)S(1)}, u32[]{:S(2)}, u32[]{:S(2)}) collective-permute-start(bf16[10,8,512]{2,1,0:T(8,128)(2,1)S(1)} %get-tuple-element.24), channel_id=1, source_target_pairs={{0,8},{4,12},{8,0},{12,4},{1,9},{5,13},{9,1},{13,5},{2,10},{6,14},... | collective-permute-start | bytes 245768 | tf_op jit(solution)/shard_map/ppermute | solution.py:352
  12.5 6.9 %collective-permute-start.4 = (bf16[10,8,512]{2,1,0:T(8,128)(2,1)S(1)}, bf16[10,8,512]{2,1,0:T(8,128)(2,1)S(1)}, u32[]{:S(2)}, u32[]{:S(2)}) collective-permute-start(bf16[10,8,512]{2,1,0:T(8,128)(2,1)S(1)} %get-tuple-element.25), channel_id=1, source_target_pairs={{0,12},{4,0},{8,4},{12,8},{1,13},{5,1},{9,5},{13,9},{2,14},{6,2},{... | collective-permute-start | bytes 245768 | tf_op jit(solution)/shard_map/ppermute | solution.py:352
  15.1 4.2 %copy-start.2 = (bf16[256,256]{1,0:T(8,128)(2,1)S(1)}, bf16[256,256]{1,0:T(8,128)(2,1)}, u32[]{:S(2)}) copy-start(bf16[256,256]{1,0:T(8,128)(2,1)} %prefix_keys.1) | copy-start | bytes 393220
  15.1 4.2 %copy-start.3 = (bf16[256,256]{1,0:T(8,128)(2,1)S(1)}, bf16[256,256]{1,0:T(8,128)(2,1)}, u32[]{:S(2)}) copy-start(bf16[256,256]{1,0:T(8,128)(2,1)} %prefix_values.1) | copy-start | bytes 393220
  16.0 5.7 %collective-permute-start.5 = (bf16[32,256]{1,0:T(8,128)(2,1)S(1)}, bf16[32,256]{1,0:T(8,128)(2,1)S(1)}, u32[]{:S(2)}, u32[]{:S(2)}) collective-permute-start(bf16[32,256]{1,0:T(8,128)(2,1)S(1)} %get-tuple-element.29), channel_id=1, source_target_pairs={{0,1},{1,2},{2,3},{3,0},{4,5},{5,6},{6,7},{7,4},{8,9},{9,10},{10,1... | collective-permute-start | bytes 49160 | tf_op jit(solution)/shard_map/ppermute | solution.py:352
  16.1 5.6 %collective-permute-start.6 = (bf16[32,256]{1,0:T(8,128)(2,1)S(1)}, bf16[32,256]{1,0:T(8,128)(2,1)S(1)}, u32[]{:S(2)}, u32[]{:S(2)}) collective-permute-start(bf16[32,256]{1,0:T(8,128)(2,1)S(1)} %get-tuple-element.30), channel_id=1, source_target_pairs={{0,2},{1,3},{2,0},{3,1},{4,6},{5,7},{6,4},{7,5},{8,10},{9,11},{10,... | collective-permute-start | bytes 49160 | tf_op jit(solution)/shard_map/ppermute | solution.py:352
  17.7 4.1 %collective-permute-start.7 = (bf16[32,256]{1,0:T(8,128)(2,1)S(1)}, bf16[32,256]{1,0:T(8,128)(2,1)S(1)}, u32[]{:S(2)}, u32[]{:S(2)}) collective-permute-start(bf16[32,256]{1,0:T(8,128)(2,1)S(1)} %get-tuple-element.31), channel_id=1, source_target_pairs={{0,3},{1,0},{2,1},{3,2},{4,7},{5,4},{6,5},{7,6},{8,11},{9,8},{10,9... | collective-permute-start | bytes 49160 | tf_op jit(solution)/shard_map/ppermute | solution.py:352

commit v4 on v3

--- a/solution.py
+++ b/solution.py
@@ -428,7 +428,7 @@
     pages_only.insert(JOINED, own[JOINED])
     handed = shifted(pages_only, "group")
     later = [distance for distance in range(1, groups) if distance != JOINED]
-    held = dict(zip(later, after([own[distance] for distance in later], [*handed[1:], plan])))
+    held = dict(zip(later, after([own[distance] for distance in later], [*(handed[n] for n in later), plan])))
     moved = shifted([own[0]] + [held.get(distance) for distance in range(1, groups)], "group")
     arrived = [handed[n] if n == JOINED else moved[n] for n in range(groups)]
 

time: 22.5 us -> 22.5 us (level)
  no operation moved by 1% of the time
where the time goes in v4:
time: 22.5 us; the launch traced here: 22.3 us
  starting transfers between devices  13.4 us (60%)
  Pallas kernels  6.69 us (30%)
  waiting for transfers between devices  1.41 us (6%)
  between operations  0.73 us (3%)
    ppermute x8, starting transfers between devices, shifted(): lax.ppermute(chunks[d], axis, [(i, (i + d) % size) for i in range(size)])  13.4 us
    pallas_call x1, Pallas kernels, per_device(): pl.pallas_call(functools.partial(attention_kernel, groups, heads_q, heads...  2.34 us
    pallas_call x1, Pallas kernels, per_device(): pl.pallas_call(functools.partial(plan_kernel, groups, tensors), out_shape...  1.72 us
    ppermute x8, waiting for transfers between devices, shifted(): lax.ppermute(chunks[d], axis, [(i, (i + d) % size) for i in range(size)])  1.41 us
    pallas_call x1, Pallas kernels, per_device(): pl.pallas_call(functools.partial(dispatch_kernel, groups), out_shape=[chu...  1.12 us
    pallas_call x1, Pallas kernels, per_device(): pl.pallas_call(functools.partial(pages_kernel, groups, tensors), out_shap...  0.83 us
    pallas_call x1, Pallas kernels, per_device(): pl.pallas_call(functools.partial(cache_kernel, tensors), out_shape=jax.Sh...  0.69 us
  transfers between devices with their start and end apart: 8, of which 3 were waited for; matrix products, arithmetic and copies ran while one was open for 0% of the time, Pallas kernels for 22%

profile of v4, /device:TPU:0, one launch (start us, length us, event | category | flops | bytes accessed | tf_op | source)
XLA Modules:
  0.0 22.3 jit_solution(2331173215666001715)
XLA Ops:
  0.6 1.1 %dispatch.1 = (bf16[10,8,512]{2,1,0:T(8,128)(2,1)S(1)}, bf16[14,8,512]{2,1,0:T(8,128)(2,1)S(1)}, bf16[10,8,512]{2,1,0:T(8,128)(2,1)S(1)}, bf16[10,8,512]{2,1,0:T...) custom-call(s32[4]{0:T(128)} %spread.1, ...), custom_call_target="tpu_custom_call" | custom-call | tf_op jit(solution)/shard_map/dispatch/pallas_call | solution.py:393
  1.8 0.0 copy-start.7
  1.8 3.1 %collective-permute-start = (bf16[14,8,512]{2,1,0:T(8,128)(2,1)S(1)}, bf16[14,8,512]{2,1,0:T(8,128)(2,1)S(1)}, u32[]{:S(2)}, u32[]{:S(2)}) collective-permute-start(bf16[14,8,512]{2,1,0:T(8,128)(2,1)S(1)} %get-tuple-element.19), channel_id=1, source_target_pairs={{0,4},{4,8},{8,12},{12,0},{1,5},{5,9},{9,13},{13,1},{2,6},{6,10},{... | collective-permute-start | bytes 344072 | tf_op jit(solution)/shard_map/ppermute | solution.py:352
  4.9 2.6 %collective-permute-start.1 = (bf16[4,8,512]{2,1,0:T(8,128)(2,1)S(1)}, bf16[4,8,512]{2,1,0:T(8,128)(2,1)S(1)}, u32[]{:S(2)}, u32[]{:S(2)}) collective-permute-start(bf16[4,8,512]{2,1,0:T(8,128)(2,1)S(1)} %get-tuple-element.22), channel_id=1, source_target_pairs={{0,8},{4,12},{8,0},{12,4},{1,9},{5,13},{9,1},{13,5},{2,10},{6,14},... | collective-permute-start | bytes 98312 | tf_op jit(solution)/shard_map/ppermute | solution.py:352
  7.4 1.3 %collective-permute-start.2 = (bf16[4,8,512]{2,1,0:T(8,128)(2,1)S(1)}, bf16[4,8,512]{2,1,0:T(8,128)(2,1)S(1)}, u32[]{:S(2)}, u32[]{:S(2)}) collective-permute-start(bf16[4,8,512]{2,1,0:T(8,128)(2,1)S(1)} %get-tuple-element.23), channel_id=1, source_target_pairs={{0,12},{4,0},{8,4},{12,8},{1,13},{5,1},{9,5},{13,9},{2,14},{6,2},{... | collective-permute-start | bytes 98312 | tf_op jit(solution)/shard_map/ppermute | solution.py:352
  8.8 1.7 %plan.1 = (s32[7,9]{1,0:T(8,128)S(1)}, bf16[128,128]{1,0:T(8,128)(2,1)S(1)}) custom-call(s32[4]{0:T(128)S(1)} %copy-done.6, s32[4,4]{1,0:T(4,128)S(1)} %copy-done.4, s32[4,4]{1,0:T(4,128)S(1)} %copy-done.7, s32[4,4]{1,0:T(4,128)S(1)} %copy-done.5, s32[4,4]{1,0:T(4,128)S(1)} %copy-done.8, bf16[10,8,512]{2,1,0:T(8,128)(2,1)S(1)} %get-tuple-element.17._.rest_0_), custom_call_target="tpu_custom_call" | custom-call | tf_op jit(solution)/shard_map/plan/pallas_call | solution.py:416
  10.5 1.0 %collective-permute-done.1.refs_2_.rest_2_ = bf16[4,8,512]{2,1,0:T(8,128)(2,1)S(1)} collective-permute-done((bf16[4,8,512]{2,1,0:T(8,128)(2,1)S(1)}, bf16[4,8,512]{2,1,0:T(8,128)(2,1)S(1)}, u32[]{:S(2)}, u32[]{:S(2)}) %collective-permute-start.1) | collective-permute-done | bytes 32800 | tf_op jit(solution)/shard_map/ppermute | solution.py:352
  11.5 0.1 collective-permute-done.2.refs_3_.rest_3_
  11.7 0.8 %collective-permute-start.3 = (bf16[10,8,512]{2,1,0:T(8,128)(2,1)S(1)}, bf16[10,8,512]{2,1,0:T(8,128)(2,1)S(1)}, u32[]{:S(2)}, u32[]{:S(2)}) collective-permute-start(bf16[10,8,512]{2,1,0:T(8,128)(2,1)S(1)} %get-tuple-element.24), channel_id=1, source_target_pairs={{0,8},{4,12},{8,0},{12,4},{1,9},{5,13},{9,1},{13,5},{2,10},{6,14},... | collective-permute-start | bytes 245768 | tf_op jit(solution)/shard_map/ppermute | solution.py:352
  12.4 2.6 %collective-permute-start.4 = (bf16[10,8,512]{2,1,0:T(8,128)(2,1)S(1)}, bf16[10,8,512]{2,1,0:T(8,128)(2,1)S(1)}, u32[]{:S(2)}, u32[]{:S(2)}) collective-permute-start(bf16[10,8,512]{2,1,0:T(8,128)(2,1)S(1)} %get-tuple-element.25), channel_id=1, source_target_pairs={{0,12},{4,0},{8,4},{12,8},{1,13},{5,1},{9,5},{13,9},{2,14},{6,2},{... | collective-permute-start | bytes 245768 | tf_op jit(solution)/shard_map/ppermute | solution.py:352
  15.1 0.0 collective-permute-done.rest_1_
  15.1 0.0 copy-start.2
  15.1 0.0 copy-start.3
  15.1 0.8 %finish_pages.1 = (bf16[32,256]{1,0:T(8,128)(2,1)S(1)}, bf16[32,256]{1,0:T(8,128)(2,1)S(1)}, bf16[32,256]{1,0:T(8,128)(2,1)S(1)}, bf16[32,256]{1,0:T(8,128)(2,1)S(1)}) custom-call(s32[7,9]{1,0:T(8,128)S(1)} %get-tuple-element.18.refs_4_.plan, bf16[128,128]{1,0:T(8,128)(2,1)S(1)} %get-tuple-element.26.pick, f32[80,128]{1,0:T(8,128)S(1)} %copy-done.1, ...), custom_call_target="tpu_custom_call" | custom-call | tf_op jit(solution)/shard_map/finish_pages/pallas_call | solution.py:436
  15.9 0.1 collective-permute-start.5
  16.0 1.6 %collective-permute-start.6 = (bf16[32,256]{1,0:T(8,128)(2,1)S(1)}, bf16[32,256]{1,0:T(8,128)(2,1)S(1)}, u32[]{:S(2)}, u32[]{:S(2)}) collective-permute-start(bf16[32,256]{1,0:T(8,128)(2,1)S(1)} %get-tuple-element.30), channel_id=1, source_target_pairs={{0,2},{1,3},{2,0},{3,1},{4,6},{5,7},{6,4},{7,5},{8,10},{9,11},{10,... | collective-permute-start | bytes 49160 | tf_op jit(solution)/shard_map/ppermute | solution.py:352
  17.6 1.4 %collective-permute-start.7 = (bf16[32,256]{1,0:T(8,128)(2,1)S(1)}, bf16[32,256]{1,0:T(8,128)(2,1)S(1)}, u32[]{:S(2)}, u32[]{:S(2)}) collective-permute-start(bf16[32,256]{1,0:T(8,128)(2,1)S(1)} %get-tuple-element.31), channel_id=1, source_target_pairs={{0,3},{1,0},{2,1},{3,2},{4,7},{5,4},{6,5},{7,6},{8,11},{9,8},{10,9... | collective-permute-start | bytes 49160 | tf_op jit(solution)/shard_map/ppermute | solution.py:352
  19.0 0.3 %collective-permute-done.3.rest_2_ = bf16[10,8,512]{2,1,0:T(8,128)(2,1)S(1)} collective-permute-done((bf16[10,8,512]{2,1,0:T(8,128)(2,1)S(1)}, bf16[10,8,512]{2,1,0:T(8,128)(2,1)S(1)}, u32[]{:S(2)}, u32[]{:S(2)}) %collective-permute-start.3) | collective-permute-done | bytes 81952 | tf_op jit(solution)/shard_map/ppermute | solution.py:352
  19.3 0.0 collective-permute-done.4.rest_3_
  19.3 2.3 %attention.1.rest_4_ = bf16[8,8,2048]{2,1,0:T(8,128)(2,1)} custom-call(s32[7,9]{1,0:T(8,128)S(1)} %get-tuple-element.18.refs_4_.plan, bf16[256,256]{1,0:T(8,128)(2,1)S(1)} %copy-done.2, bf16[256,256]{1,0:T(8,128)(2,1)S(1)} %copy-done.3, f32[80,128]{1,0:T(8,128)S(1)} %copy-done.1, f32[80,128]{1,0:T(8,128)S(1)} %copy-done, ...), custom_call_target="tpu_custom_call" | custom-call | tf_op jit(solution)/shard_map/attention/pallas_call | solution.py:450
  21.6 0.0 collective-permute-done.5.rest_1_
  21.6 0.0 collective-permute-done.6.rest_2_
  21.6 0.0 collective-permute-done.7.rest_3_
  21.6 0.7 %place_pages.1 = bf16[16,2,1024]{2,1,0:T(2,128)(2,1)} custom-call(bf16[32,256]{1,0:T(8,128)(2,1)S(1)} %get-tuple-element.28.rest_0_, bf16[32,256]{1,0:T(8,128)(2,1)S(1)} %collective-permute-done.5.rest_1_, bf16[32,256]{1,0:T(8,128)(2,1)S(1)} %collective-permute-done.6.rest_2_, bf16[32,256]{1,0:T(8,128)(2,1)S(1)} %collective-permute-done.7.rest_3_, ...), custom_call_target="tpu_custom_call" | custom-call | tf_op jit(solution)/shard_map/place_pages/pallas_call | solution.py:460
  (16 shorter events, 0.0 us)
Async XLA Ops:
  0.6 8.2 %copy-start.8 = (s32[4,4]{1,0:T(4,128)S(1)}, s32[4,4]{1,0:T(4,128)}, u32[]{:S(2)}) copy-start(s32[4,4]{1,0:T(4,128)} %page_start.1) | copy-start | bytes 196
  1.8 7.0 %copy-start.7 = (s32[4,4]{1,0:T(4,128)S(1)}, s32[4,4]{1,0:T(4,128)}, u32[]{:S(2)}) copy-start(s32[4,4]{1,0:T(4,128)} %prefix_len.1) | copy-start | bytes 196
  1.8 13.3 %collective-permute-start = (bf16[14,8,512]{2,1,0:T(8,128)(2,1)S(1)}, bf16[14,8,512]{2,1,0:T(8,128)(2,1)S(1)}, u32[]{:S(2)}, u32[]{:S(2)}) collective-permute-start(bf16[14,8,512]{2,1,0:T(8,128)(2,1)S(1)} %get-tuple-element.19), channel_id=1, source_target_pairs={{0,4},{4,8},{8,12},{12,0},{1,5},{5,9},{9,13},{13,1},{2,6},{6,10},{... | collective-permute-start | bytes 344072 | tf_op jit(solution)/shard_map/ppermute | solution.py:352
  4.9 4.0 %copy-start.5 = (s32[4,4]{1,0:T(4,128)S(1)}, s32[4,4]{1,0:T(4,128)}, u32[]{:S(2)}) copy-start(s32[4,4]{1,0:T(4,128)} %owner.1) | copy-start | bytes 196
  4.9 4.0 %copy-start.4 = (s32[4,4]{1,0:T(4,128)S(1)}, s32[4,4]{1,0:T(4,128)}, u32[]{:S(2)}) copy-start(s32[4,4]{1,0:T(4,128)} %new_blocks.1) | copy-start | bytes 196
  4.9 6.7 %collective-permute-start.1 = (bf16[4,8,512]{2,1,0:T(8,128)(2,1)S(1)}, bf16[4,8,512]{2,1,0:T(8,128)(2,1)S(1)}, u32[]{:S(2)}, u32[]{:S(2)}) collective-permute-start(bf16[4,8,512]{2,1,0:T(8,128)(2,1)S(1)} %get-tuple-element.22), channel_id=1, source_target_pairs={{0,8},{4,12},{8,0},{12,4},{1,9},{5,13},{9,1},{13,5},{2,10},{6,14},... | collective-permute-start | bytes 98312 | tf_op jit(solution)/shard_map/ppermute | solution.py:352
  7.4 1.4 %copy-start.6 = (s32[4]{0:T(128)S(1)}, s32[4]{0:T(128)}, u32[]{:S(2)}) copy-start(s32[4]{0:T(128)} %spread.1) | copy-start | bytes 52
  7.4 4.2 %collective-permute-start.2 = (bf16[4,8,512]{2,1,0:T(8,128)(2,1)S(1)}, bf16[4,8,512]{2,1,0:T(8,128)(2,1)S(1)}, u32[]{:S(2)}, u32[]{:S(2)}) collective-permute-start(bf16[4,8,512]{2,1,0:T(8,128)(2,1)S(1)} %get-tuple-element.23), channel_id=1, source_target_pairs={{0,12},{4,0},{8,4},{12,8},{1,13},{5,1},{9,5},{13,9},{2,14},{6,2},{... | collective-permute-start | bytes 98312 | tf_op jit(solution)/shard_map/ppermute | solution.py:352
  11.7 3.4 %copy-start = (f32[80,128]{1,0:T(8,128)S(1)}, f32[80,128]{1,0:T(8,128)}, u32[]{:S(2)}) copy-start(f32[80,128]{1,0:T(8,128)} %constant.5.clone.sine) | copy-start | bytes 122884
  11.7 3.4 %copy-start.1 = (f32[80,128]{1,0:T(8,128)S(1)}, f32[80,128]{1,0:T(8,128)}, u32[]{:S(2)}) copy-start(f32[80,128]{1,0:T(8,128)} %constant.4.clone.cosine) | copy-start | bytes 122884
  11.7 7.6 %collective-permute-start.3 = (bf16[10,8,512]{2,1,0:T(8,128)(2,1)S(1)}, bf16[10,8,512]{2,1,0:T(8,128)(2,1)S(1)}, u32[]{:S(2)}, u32[]{:S(2)}) collective-permute-start(bf16[10,8,512]{2,1,0:T(8,128)(2,1)S(1)} %get-tuple-element.24), channel_id=1, source_target_pairs={{0,8},{4,12},{8,0},{12,4},{1,9},{5,13},{9,1},{13,5},{2,10},{6,14},... | collective-permute-start | bytes 245768 | tf_op jit(solution)/shard_map/ppermute | solution.py:352
  12.4 6.8 %collective-permute-start.4 = (bf16[10,8,512]{2,1,0:T(8,128)(2,1)S(1)}, bf16[10,8,512]{2,1,0:T(8,128)(2,1)S(1)}, u32[]{:S(2)}, u32[]{:S(2)}) collective-permute-start(bf16[10,8,512]{2,1,0:T(8,128)(2,1)S(1)} %get-tuple-element.25), channel_id=1, source_target_pairs={{0,12},{4,0},{8,4},{12,8},{1,13},{5,1},{9,5},{13,9},{2,14},{6,2},{... | collective-permute-start | bytes 245768 | tf_op jit(solution)/shard_map/ppermute | solution.py:352
  15.1 4.2 %copy-start.2 = (bf16[256,256]{1,0:T(8,128)(2,1)S(1)}, bf16[256,256]{1,0:T(8,128)(2,1)}, u32[]{:S(2)}) copy-start(bf16[256,256]{1,0:T(8,128)(2,1)} %prefix_keys.1) | copy-start | bytes 393220
  15.1 4.2 %copy-start.3 = (bf16[256,256]{1,0:T(8,128)(2,1)S(1)}, bf16[256,256]{1,0:T(8,128)(2,1)}, u32[]{:S(2)}) copy-start(bf16[256,256]{1,0:T(8,128)(2,1)} %prefix_values.1) | copy-start | bytes 393220
  15.9 5.7 %collective-permute-start.5 = (bf16[32,256]{1,0:T(8,128)(2,1)S(1)}, bf16[32,256]{1,0:T(8,128)(2,1)S(1)}, u32[]{:S(2)}, u32[]{:S(2)}) collective-permute-start(bf16[32,256]{1,0:T(8,128)(2,1)S(1)} %get-tuple-element.29), channel_id=1, source_target_pairs={{0,1},{1,2},{2,3},{3,0},{4,5},{5,6},{6,7},{7,4},{8,9},{9,10},{10,1... | collective-permute-start | bytes 49160 | tf_op jit(solution)/shard_map/ppermute | solution.py:352
  16.0 5.6 %collective-permute-start.6 = (bf16[32,256]{1,0:T(8,128)(2,1)S(1)}, bf16[32,256]{1,0:T(8,128)(2,1)S(1)}, u32[]{:S(2)}, u32[]{:S(2)}) collective-permute-start(bf16[32,256]{1,0:T(8,128)(2,1)S(1)} %get-tuple-element.30), channel_id=1, source_target_pairs={{0,2},{1,3},{2,0},{3,1},{4,6},{5,7},{6,4},{7,5},{8,10},{9,11},{10,... | collective-permute-start | bytes 49160 | tf_op jit(solution)/shard_map/ppermute | solution.py:352
  17.6 4.0 %collective-permute-start.7 = (bf16[32,256]{1,0:T(8,128)(2,1)S(1)}, bf16[32,256]{1,0:T(8,128)(2,1)S(1)}, u32[]{:S(2)}, u32[]{:S(2)}) collective-permute-start(bf16[32,256]{1,0:T(8,128)(2,1)S(1)} %get-tuple-element.31), channel_id=1, source_target_pairs={{0,3},{1,0},{2,1},{3,2},{4,7},{5,4},{6,5},{7,6},{8,11},{9,8},{10,9... | collective-permute-start | bytes 49160 | tf_op jit(solution)/shard_map/ppermute | solution.py:352

commit v5 on v4

--- a/solution.py
+++ b/solution.py
@@ -18,7 +18,7 @@
 
 SMEM = pl.BlockSpec(memory_space=pltpu.SMEM)
 VMEM = pl.BlockSpec(memory_space=pltpu.VMEM)
-JOINED = 1
+JOINED = 2
 PROMPT, OFFSET, LIVE, CACHED, SOURCE, COLUMN, PLACE = range(7)
 ANY = pl.BlockSpec(memory_space=pl.ANY)
 HBM = pl.BlockSpec(memory_space=pltpu.HBM)

time: 22.5 us -> 23.6 us (1.049)
  starting transfers between devices: 13.4 us -> 15.3 us
  waiting for transfers between devices: 1.41 us -> 0.72 us
    ppermute x8, starting transfers between devices: 13.4 us -> 15.3 us  [shifted(): lax.ppermute(chunks[d], axis, [(i, (i + d) % size) for i in range(size)])]
    ppermute x8, waiting for transfers between devices: 1.41 us -> 0.72 us  [shifted(): lax.ppermute(chunks[d], axis, [(i, (i + d) % size) for i in range(size)])]
  transfers between devices with their start and end apart: 8 -> 8, of which waited for: 3 -> 2; matrix products, arithmetic and copies ran while one was open for 0% -> 0% of each run, Pallas kernels for 22% -> 21%
where the time goes in v5:
time: 23.6 us; the launch traced here: 23.5 us
  starting transfers between devices  15.3 us (65%)
  Pallas kernels  6.69 us (28%)
  between operations  0.74 us (3%)
  waiting for transfers between devices  0.72 us (3%)
    ppermute x8, starting transfers between devices, shifted(): lax.ppermute(chunks[d], axis, [(i, (i + d) % size) for i in range(size)])  15.3 us
    pallas_call x1, Pallas kernels, per_device(): pl.pallas_call(functools.partial(attention_kernel, groups, heads_q, heads...  2.33 us
    pallas_call x1, Pallas kernels, per_device(): pl.pallas_call(functools.partial(plan_kernel, groups, tensors), out_shape...  1.72 us
    pallas_call x1, Pallas kernels, per_device(): pl.pallas_call(functools.partial(dispatch_kernel, groups), out_shape=[chu...  1.11 us
    pallas_call x1, Pallas kernels, per_device(): pl.pallas_call(functools.partial(pages_kernel, groups, tensors), out_shap...  0.83 us
    ppermute x8, waiting for transfers between devices, shifted(): lax.ppermute(chunks[d], axis, [(i, (i + d) % size) for i in range(size)])  0.72 us
    pallas_call x1, Pallas kernels, per_device(): pl.pallas_call(functools.partial(cache_kernel, tensors), out_shape=jax.Sh...  0.69 us
  transfers between devices with their start and end apart: 8, of which 2 were waited for; matrix products, arithmetic and copies ran while one was open for 0% of the time, Pallas kernels for 21%

profile of v5, /device:TPU:0, one launch (start us, length us, event | category | flops | bytes accessed | tf_op | source)
XLA Modules:
  0.0 23.5 jit_solution(3799379701217834213)
XLA Ops:
  0.6 1.1 %dispatch.1 = (bf16[10,8,512]{2,1,0:T(8,128)(2,1)S(1)}, bf16[10,8,512]{2,1,0:T(8,128)(2,1)S(1)}, bf16[14,8,512]{2,1,0:T(8,128)(2,1)S(1)}, bf16[10,8,512]{2,1,0:T...) custom-call(s32[4]{0:T(128)} %spread.1, ...), custom_call_target="tpu_custom_call" | custom-call | tf_op jit(solution)/shard_map/dispatch/pallas_call | solution.py:393
  1.8 0.0 copy-start.7
  1.8 4.1 %collective-permute-start.3 = (bf16[14,8,512]{2,1,0:T(8,128)(2,1)S(1)}, bf16[14,8,512]{2,1,0:T(8,128)(2,1)S(1)}, u32[]{:S(2)}, u32[]{:S(2)}) collective-permute-start(bf16[14,8,512]{2,1,0:T(8,128)(2,1)S(1)} %get-tuple-element.24), channel_id=1, source_target_pairs={{0,8},{4,12},{8,0},{12,4},{1,9},{5,13},{9,1},{13,5},{2,10},{6,14},... | collective-permute-start | bytes 344072 | tf_op jit(solution)/shard_map/ppermute | solution.py:352
  5.9 1.6 %collective-permute-start = (bf16[4,8,512]{2,1,0:T(8,128)(2,1)S(1)}, bf16[4,8,512]{2,1,0:T(8,128)(2,1)S(1)}, u32[]{:S(2)}, u32[]{:S(2)}) collective-permute-start(bf16[4,8,512]{2,1,0:T(8,128)(2,1)S(1)} %get-tuple-element.21), channel_id=1, source_target_pairs={{0,4},{4,8},{8,12},{12,0},{1,5},{5,9},{9,13},{13,1},{2,6},{6,10},{... | collective-permute-start | bytes 98312 | tf_op jit(solution)/shard_map/ppermute | solution.py:352
  7.5 2.2 %collective-permute-start.1 = (bf16[4,8,512]{2,1,0:T(8,128)(2,1)S(1)}, bf16[4,8,512]{2,1,0:T(8,128)(2,1)S(1)}, u32[]{:S(2)}, u32[]{:S(2)}) collective-permute-start(bf16[4,8,512]{2,1,0:T(8,128)(2,1)S(1)} %get-tuple-element.22), channel_id=1, source_target_pairs={{0,12},{4,0},{8,4},{12,8},{1,13},{5,1},{9,5},{13,9},{2,14},{6,2},{... | collective-permute-start | bytes 98312 | tf_op jit(solution)/shard_map/ppermute | solution.py:352
  9.7 1.7 %plan.1 = (s32[7,9]{1,0:T(8,128)S(1)}, bf16[128,128]{1,0:T(8,128)(2,1)S(1)}) custom-call(s32[4]{0:T(128)S(1)} %copy-done.6, s32[4,4]{1,0:T(4,128)S(1)} %copy-done.4, s32[4,4]{1,0:T(4,128)S(1)} %copy-done.7, s32[4,4]{1,0:T(4,128)S(1)} %copy-done.5, s32[4,4]{1,0:T(4,128)S(1)} %copy-done.8, bf16[10,8,512]{2,1,0:T(8,128)(2,1)S(1)} %get-tuple-element.17._.rest_0_), custom_call_target="tpu_custom_call" | custom-call | tf_op jit(solution)/shard_map/plan/pallas_call | solution.py:416
  11.5 0.3 %collective-permute-done.refs_2_.rest_1_ = bf16[4,8,512]{2,1,0:T(8,128)(2,1)S(1)} collective-permute-done((bf16[4,8,512]{2,1,0:T(8,128)(2,1)S(1)}, bf16[4,8,512]{2,1,0:T(8,128)(2,1)S(1)}, u32[]{:S(2)}, u32[]{:S(2)}) %collective-permute-start) | collective-permute-done | bytes 32800 | tf_op jit(solution)/shard_map/ppermute | solution.py:352
  11.8 0.4 %collective-permute-done.1.refs_3_.rest_3_ = bf16[4,8,512]{2,1,0:T(8,128)(2,1)S(1)} collective-permute-done((bf16[4,8,512]{2,1,0:T(8,128)(2,1)S(1)}, bf16[4,8,512]{2,1,0:T(8,128)(2,1)S(1)}, u32[]{:S(2)}, u32[]{:S(2)}) %collective-permute-start.1) | collective-permute-done | bytes 32800 | tf_op jit(solution)/shard_map/ppermute | solution.py:352
  12.2 1.5 %collective-permute-start.2 = (bf16[10,8,512]{2,1,0:T(8,128)(2,1)S(1)}, bf16[10,8,512]{2,1,0:T(8,128)(2,1)S(1)}, u32[]{:S(2)}, u32[]{:S(2)}) collective-permute-start(bf16[10,8,512]{2,1,0:T(8,128)(2,1)S(1)} %get-tuple-element.23), channel_id=1, source_target_pairs={{0,4},{4,8},{8,12},{12,0},{1,5},{5,9},{9,13},{13,1},{2,6},{6,10},{... | collective-permute-start | bytes 245768 | tf_op jit(solution)/shard_map/ppermute | solution.py:352
  13.7 2.3 %collective-permute-start.4 = (bf16[10,8,512]{2,1,0:T(8,128)(2,1)S(1)}, bf16[10,8,512]{2,1,0:T(8,128)(2,1)S(1)}, u32[]{:S(2)}, u32[]{:S(2)}) collective-permute-start(bf16[10,8,512]{2,1,0:T(8,128)(2,1)S(1)} %get-tuple-element.25), channel_id=1, source_target_pairs={{0,12},{4,0},{8,4},{12,8},{1,13},{5,1},{9,5},{13,9},{2,14},{6,2},{... | collective-permute-start | bytes 245768 | tf_op jit(solution)/shard_map/ppermute | solution.py:352
  16.0 0.0 collective-permute-done.3.rest_2_
  16.0 0.0 copy-start.2
  16.0 0.0 copy-start.3
  16.0 0.8 %finish_pages.1 = (bf16[32,256]{1,0:T(8,128)(2,1)S(1)}, bf16[32,256]{1,0:T(8,128)(2,1)S(1)}, bf16[32,256]{1,0:T(8,128)(2,1)S(1)}, bf16[32,256]{1,0:T(8,128)(2,1)S(1)}) custom-call(s32[7,9]{1,0:T(8,128)S(1)} %get-tuple-element.18.refs_4_.plan, bf16[128,128]{1,0:T(8,128)(2,1)S(1)} %get-tuple-element.26.pick, f32[80,128]{1,0:T(8,128)S(1)} %copy-done.1, ...), custom_call_target="tpu_custom_call" | custom-call | tf_op jit(solution)/shard_map/finish_pages/pallas_call | solution.py:436
  16.9 0.1 collective-permute-start.5
  16.9 2.1 %collective-permute-start.6 = (bf16[32,256]{1,0:T(8,128)(2,1)S(1)}, bf16[32,256]{1,0:T(8,128)(2,1)S(1)}, u32[]{:S(2)}, u32[]{:S(2)}) collective-permute-start(bf16[32,256]{1,0:T(8,128)(2,1)S(1)} %get-tuple-element.30), channel_id=1, source_target_pairs={{0,2},{1,3},{2,0},{3,1},{4,6},{5,7},{6,4},{7,5},{8,10},{9,11},{10,... | collective-permute-start | bytes 49160 | tf_op jit(solution)/shard_map/ppermute | solution.py:352
  19.0 1.4 %collective-permute-start.7 = (bf16[32,256]{1,0:T(8,128)(2,1)S(1)}, bf16[32,256]{1,0:T(8,128)(2,1)S(1)}, u32[]{:S(2)}, u32[]{:S(2)}) collective-permute-start(bf16[32,256]{1,0:T(8,128)(2,1)S(1)} %get-tuple-element.31), channel_id=1, source_target_pairs={{0,3},{1,0},{2,1},{3,2},{4,7},{5,4},{6,5},{7,6},{8,11},{9,8},{10,9... | collective-permute-start | bytes 49160 | tf_op jit(solution)/shard_map/ppermute | solution.py:352
  20.4 0.0 collective-permute-done.2.rest_1_
  20.4 0.0 collective-permute-done.4.rest_3_
  20.5 2.3 %attention.1.rest_4_ = bf16[8,8,2048]{2,1,0:T(8,128)(2,1)} custom-call(s32[7,9]{1,0:T(8,128)S(1)} %get-tuple-element.18.refs_4_.plan, bf16[256,256]{1,0:T(8,128)(2,1)S(1)} %copy-done.2, bf16[256,256]{1,0:T(8,128)(2,1)S(1)} %copy-done.3, f32[80,128]{1,0:T(8,128)S(1)} %copy-done.1, f32[80,128]{1,0:T(8,128)S(1)} %copy-done, ...), custom_call_target="tpu_custom_call" | custom-call | tf_op jit(solution)/shard_map/attention/pallas_call | solution.py:450
  22.8 0.0 collective-permute-done.5.rest_1_
  22.8 0.0 collective-permute-done.6.rest_2_
  22.8 0.0 collective-permute-done.7.rest_3_
  22.8 0.7 %place_pages.1 = bf16[16,2,1024]{2,1,0:T(2,128)(2,1)} custom-call(bf16[32,256]{1,0:T(8,128)(2,1)S(1)} %get-tuple-element.28.rest_0_, bf16[32,256]{1,0:T(8,128)(2,1)S(1)} %collective-permute-done.5.rest_1_, bf16[32,256]{1,0:T(8,128)(2,1)S(1)} %collective-permute-done.6.rest_2_, bf16[32,256]{1,0:T(8,128)(2,1)S(1)} %collective-permute-done.7.rest_3_, ...), custom_call_target="tpu_custom_call" | custom-call | tf_op jit(solution)/shard_map/place_pages/pallas_call | solution.py:460
  (16 shorter events, 0.0 us)
Async XLA Ops:
  0.6 9.1 %copy-start.8 = (s32[4,4]{1,0:T(4,128)S(1)}, s32[4,4]{1,0:T(4,128)}, u32[]{:S(2)}) copy-start(s32[4,4]{1,0:T(4,128)} %page_start.1) | copy-start | bytes 196
  1.8 8.0 %copy-start.7 = (s32[4,4]{1,0:T(4,128)S(1)}, s32[4,4]{1,0:T(4,128)}, u32[]{:S(2)}) copy-start(s32[4,4]{1,0:T(4,128)} %prefix_len.1) | copy-start | bytes 196
  1.8 14.2 %collective-permute-start.3 = (bf16[14,8,512]{2,1,0:T(8,128)(2,1)S(1)}, bf16[14,8,512]{2,1,0:T(8,128)(2,1)S(1)}, u32[]{:S(2)}, u32[]{:S(2)}) collective-permute-start(bf16[14,8,512]{2,1,0:T(8,128)(2,1)S(1)} %get-tuple-element.24), channel_id=1, source_target_pairs={{0,8},{4,12},{8,0},{12,4},{1,9},{5,13},{9,1},{13,5},{2,10},{6,14},... | collective-permute-start | bytes 344072 | tf_op jit(solution)/shard_map/ppermute | solution.py:352
  5.9 3.8 %copy-start.5 = (s32[4,4]{1,0:T(4,128)S(1)}, s32[4,4]{1,0:T(4,128)}, u32[]{:S(2)}) copy-start(s32[4,4]{1,0:T(4,128)} %owner.1) | copy-start | bytes 196
  5.9 3.8 %copy-start.4 = (s32[4,4]{1,0:T(4,128)S(1)}, s32[4,4]{1,0:T(4,128)}, u32[]{:S(2)}) copy-start(s32[4,4]{1,0:T(4,128)} %new_blocks.1) | copy-start | bytes 196
  5.9 5.9 %collective-permute-start = (bf16[4,8,512]{2,1,0:T(8,128)(2,1)S(1)}, bf16[4,8,512]{2,1,0:T(8,128)(2,1)S(1)}, u32[]{:S(2)}, u32[]{:S(2)}) collective-permute-start(bf16[4,8,512]{2,1,0:T(8,128)(2,1)S(1)} %get-tuple-element.21), channel_id=1, source_target_pairs={{0,4},{4,8},{8,12},{12,0},{1,5},{5,9},{9,13},{13,1},{2,6},{6,10},{... | collective-permute-start | bytes 98312 | tf_op jit(solution)/shard_map/ppermute | solution.py:352
  7.5 2.3 %copy-start.6 = (s32[4]{0:T(128)S(1)}, s32[4]{0:T(128)}, u32[]{:S(2)}) copy-start(s32[4]{0:T(128)} %spread.1) | copy-start | bytes 52
  7.5 4.7 %collective-permute-start.1 = (bf16[4,8,512]{2,1,0:T(8,128)(2,1)S(1)}, bf16[4,8,512]{2,1,0:T(8,128)(2,1)S(1)}, u32[]{:S(2)}, u32[]{:S(2)}) collective-permute-start(bf16[4,8,512]{2,1,0:T(8,128)(2,1)S(1)} %get-tuple-element.22), channel_id=1, source_target_pairs={{0,12},{4,0},{8,4},{12,8},{1,13},{5,1},{9,5},{13,9},{2,14},{6,2},{... | collective-permute-start | bytes 98312 | tf_op jit(solution)/shard_map/ppermute | solution.py:352
  12.2 3.8 %copy-start = (f32[80,128]{1,0:T(8,128)S(1)}, f32[80,128]{1,0:T(8,128)}, u32[]{:S(2)}) copy-start(f32[80,128]{1,0:T(8,128)} %constant.5.clone.sine) | copy-start | bytes 122884
  12.2 3.8 %copy-start.1 = (f32[80,128]{1,0:T(8,128)S(1)}, f32[80,128]{1,0:T(8,128)}, u32[]{:S(2)}) copy-start(f32[80,128]{1,0:T(8,128)} %constant.4.clone.cosine) | copy-start | bytes 122884
  12.2 8.3 %collective-permute-start.2 = (bf16[10,8,512]{2,1,0:T(8,128)(2,1)S(1)}, bf16[10,8,512]{2,1,0:T(8,128)(2,1)S(1)}, u32[]{:S(2)}, u32[]{:S(2)}) collective-permute-start(bf16[10,8,512]{2,1,0:T(8,128)(2,1)S(1)} %get-tuple-element.23), channel_id=1, source_target_pairs={{0,4},{4,8},{8,12},{12,0},{1,5},{5,9},{9,13},{13,1},{2,6},{6,10},{... | collective-permute-start | bytes 245768 | tf_op jit(solution)/shard_map/ppermute | solution.py:352
  13.7 6.8 %collective-permute-start.4 = (bf16[10,8,512]{2,1,0:T(8,128)(2,1)S(1)}, bf16[10,8,512]{2,1,0:T(8,128)(2,1)S(1)}, u32[]{:S(2)}, u32[]{:S(2)}) collective-permute-start(bf16[10,8,512]{2,1,0:T(8,128)(2,1)S(1)} %get-tuple-element.25), channel_id=1, source_target_pairs={{0,12},{4,0},{8,4},{12,8},{1,13},{5,1},{9,5},{13,9},{2,14},{6,2},{... | collective-permute-start | bytes 245768 | tf_op jit(solution)/shard_map/ppermute | solution.py:352
  16.0 4.4 %copy-start.2 = (bf16[256,256]{1,0:T(8,128)(2,1)S(1)}, bf16[256,256]{1,0:T(8,128)(2,1)}, u32[]{:S(2)}) copy-start(bf16[256,256]{1,0:T(8,128)(2,1)} %prefix_keys.1) | copy-start | bytes 393220
  16.0 4.4 %copy-start.3 = (bf16[256,256]{1,0:T(8,128)(2,1)S(1)}, bf16[256,256]{1,0:T(8,128)(2,1)}, u32[]{:S(2)}) copy-start(bf16[256,256]{1,0:T(8,128)(2,1)} %prefix_values.1) | copy-start | bytes 393220
  16.9 5.9 %collective-permute-start.5 = (bf16[32,256]{1,0:T(8,128)(2,1)S(1)}, bf16[32,256]{1,0:T(8,128)(2,1)S(1)}, u32[]{:S(2)}, u32[]{:S(2)}) collective-permute-start(bf16[32,256]{1,0:T(8,128)(2,1)S(1)} %get-tuple-element.29), channel_id=1, source_target_pairs={{0,1},{1,2},{2,3},{3,0},{4,5},{5,6},{6,7},{7,4},{8,9},{9,10},{10,1... | collective-permute-start | bytes 49160 | tf_op jit(solution)/shard_map/ppermute | solution.py:352
  16.9 5.9 %collective-permute-start.6 = (bf16[32,256]{1,0:T(8,128)(2,1)S(1)}, bf16[32,256]{1,0:T(8,128)(2,1)S(1)}, u32[]{:S(2)}, u32[]{:S(2)}) collective-permute-start(bf16[32,256]{1,0:T(8,128)(2,1)S(1)} %get-tuple-element.30), channel_id=1, source_target_pairs={{0,2},{1,3},{2,0},{3,1},{4,6},{5,7},{6,4},{7,5},{8,10},{9,11},{10,... | collective-permute-start | bytes 49160 | tf_op jit(solution)/shard_map/ppermute | solution.py:352
  19.0 3.8 %collective-permute-start.7 = (bf16[32,256]{1,0:T(8,128)(2,1)S(1)}, bf16[32,256]{1,0:T(8,128)(2,1)S(1)}, u32[]{:S(2)}, u32[]{:S(2)}) collective-permute-start(bf16[32,256]{1,0:T(8,128)(2,1)S(1)} %get-tuple-element.31), channel_id=1, source_target_pairs={{0,3},{1,0},{2,1},{3,2},{4,7},{5,4},{6,5},{7,6},{8,11},{9,8},{10,9... | collective-permute-start | bytes 49160 | tf_op jit(solution)/shard_map/ppermute | solution.py:352

commit v6 on v5

--- a/solution.py
+++ b/solution.py
@@ -18,7 +18,7 @@
 
 SMEM = pl.BlockSpec(memory_space=pltpu.SMEM)
 VMEM = pl.BlockSpec(memory_space=pltpu.VMEM)
-JOINED = 2
+JOINED = 3
 PROMPT, OFFSET, LIVE, CACHED, SOURCE, COLUMN, PLACE = range(7)
 ANY = pl.BlockSpec(memory_space=pl.ANY)
 HBM = pl.BlockSpec(memory_space=pltpu.HBM)

time: 23.6 us -> 23.9 us (1.013)
  waiting for transfers between devices: 0.72 us -> 3.71 us
  starting transfers between devices: 15.3 us -> 12.6 us
    ppermute x8, waiting for transfers between devices: 0.72 us -> 3.71 us  [shifted(): lax.ppermute(chunks[d], axis, [(i, (i + d) % size) for i in range(size)])]
    ppermute x8, starting transfers between devices: 15.3 us -> 12.6 us  [shifted(): lax.ppermute(chunks[d], axis, [(i, (i + d) % size) for i in range(size)])]
where the time goes in v6:
time: 23.9 us; the launch traced here: 23.8 us
  starting transfers between devices  12.6 us (53%)
  Pallas kernels  6.68 us (28%)
  waiting for transfers between devices  3.71 us (16%)
  between operations  0.74 us (3%)
    ppermute x8, starting transfers between devices, shifted(): lax.ppermute(chunks[d], axis, [(i, (i + d) % size) for i in range(size)])  12.6 us
    ppermute x8, waiting for transfers between devices, shifted(): lax.ppermute(chunks[d], axis, [(i, (i + d) % size) for i in range(size)])  3.71 us
    pallas_call x1, Pallas kernels, per_device(): pl.pallas_call(functools.partial(attention_kernel, groups, heads_q, heads...  2.33 us
    pallas_call x1, Pallas kernels, per_device(): pl.pallas_call(functools.partial(plan_kernel, groups, tensors), out_shape...  1.72 us
    pallas_call x1, Pallas kernels, per_device(): pl.pallas_call(functools.partial(dispatch_kernel, groups), out_shape=[chu...  1.11 us
    pallas_call x1, Pallas kernels, per_device(): pl.pallas_call(functools.partial(pages_kernel, groups, tensors), out_shap...  0.83 us
    pallas_call x1, Pallas kernels, per_device(): pl.pallas_call(functools.partial(cache_kernel, tensors), out_shape=jax.Sh...  0.69 us
  transfers between devices with their start and end apart: 8, of which 2 were waited for; matrix products, arithmetic and copies ran while one was open for 0% of the time, Pallas kernels for 21%

profile of v6, /device:TPU:0, one launch (start us, length us, event | category | flops | bytes accessed | tf_op | source)
XLA Modules:
  0.0 23.8 jit_solution(11624965516758901465)
XLA Ops:
  0.6 1.1 %dispatch.1 = (bf16[10,8,512]{2,1,0:T(8,128)(2,1)S(1)}, bf16[10,8,512]{2,1,0:T(8,128)(2,1)S(1)}, bf16[10,8,512]{2,1,0:T(8,128)(2,1)S(1)}, bf16[14,8,512]{2,1,0:T...) custom-call(s32[4]{0:T(128)} %spread.1, ...), custom_call_target="tpu_custom_call" | custom-call | tf_op jit(solution)/shard_map/dispatch/pallas_call | solution.py:393
  1.8 0.0 copy-start.7
  1.8 5.1 %collective-permute-start.4 = (bf16[14,8,512]{2,1,0:T(8,128)(2,1)S(1)}, bf16[14,8,512]{2,1,0:T(8,128)(2,1)S(1)}, u32[]{:S(2)}, u32[]{:S(2)}) collective-permute-start(bf16[14,8,512]{2,1,0:T(8,128)(2,1)S(1)} %get-tuple-element.25), channel_id=1, source_target_pairs={{0,12},{4,0},{8,4},{12,8},{1,13},{5,1},{9,5},{13,9},{2,14},{6,2},{... | collective-permute-start | bytes 344072 | tf_op jit(solution)/shard_map/ppermute | solution.py:352
  6.9 0.0 collective-permute-start
  6.9 1.0 %collective-permute-start.1 = (bf16[4,8,512]{2,1,0:T(8,128)(2,1)S(1)}, bf16[4,8,512]{2,1,0:T(8,128)(2,1)S(1)}, u32[]{:S(2)}, u32[]{:S(2)}) collective-permute-start(bf16[4,8,512]{2,1,0:T(8,128)(2,1)S(1)} %get-tuple-element.22), channel_id=1, source_target_pairs={{0,8},{4,12},{8,0},{12,4},{1,9},{5,13},{9,1},{13,5},{2,10},{6,14},... | collective-permute-start | bytes 98312 | tf_op jit(solution)/shard_map/ppermute | solution.py:352
  7.9 1.7 %plan.1 = (s32[7,9]{1,0:T(8,128)S(1)}, bf16[128,128]{1,0:T(8,128)(2,1)S(1)}) custom-call(s32[4]{0:T(128)S(1)} %copy-done.6, s32[4,4]{1,0:T(4,128)S(1)} %copy-done.4, s32[4,4]{1,0:T(4,128)S(1)} %copy-done.7, s32[4,4]{1,0:T(4,128)S(1)} %copy-done.5, s32[4,4]{1,0:T(4,128)S(1)} %copy-done.8, bf16[10,8,512]{2,1,0:T(8,128)(2,1)S(1)} %get-tuple-element.17._.rest_0_), custom_call_target="tpu_custom_call" | custom-call | tf_op jit(solution)/shard_map/plan/pallas_call | solution.py:416
  9.6 2.9 %collective-permute-done.refs_2_.rest_1_ = bf16[4,8,512]{2,1,0:T(8,128)(2,1)S(1)} collective-permute-done((bf16[4,8,512]{2,1,0:T(8,128)(2,1)S(1)}, bf16[4,8,512]{2,1,0:T(8,128)(2,1)S(1)}, u32[]{:S(2)}, u32[]{:S(2)}) %collective-permute-start) | collective-permute-done | bytes 32800 | tf_op jit(solution)/shard_map/ppermute | solution.py:352
  12.6 0.0 collective-permute-done.1.refs_3_.rest_2_
  12.6 0.9 %collective-permute-start.2 = (bf16[10,8,512]{2,1,0:T(8,128)(2,1)S(1)}, bf16[10,8,512]{2,1,0:T(8,128)(2,1)S(1)}, u32[]{:S(2)}, u32[]{:S(2)}) collective-permute-start(bf16[10,8,512]{2,1,0:T(8,128)(2,1)S(1)} %get-tuple-element.23), channel_id=1, source_target_pairs={{0,4},{4,8},{8,12},{12,0},{1,5},{5,9},{9,13},{13,1},{2,6},{6,10},{... | collective-permute-start | bytes 245768 | tf_op jit(solution)/shard_map/ppermute | solution.py:352
  13.5 2.6 %collective-permute-start.3 = (bf16[10,8,512]{2,1,0:T(8,128)(2,1)S(1)}, bf16[10,8,512]{2,1,0:T(8,128)(2,1)S(1)}, u32[]{:S(2)}, u32[]{:S(2)}) collective-permute-start(bf16[10,8,512]{2,1,0:T(8,128)(2,1)S(1)} %get-tuple-element.24), channel_id=1, source_target_pairs={{0,8},{4,12},{8,0},{12,4},{1,9},{5,13},{9,1},{13,5},{2,10},{6,14},... | collective-permute-start | bytes 245768 | tf_op jit(solution)/shard_map/ppermute | solution.py:352
  16.1 0.0 collective-permute-done.4.rest_3_
  16.1 0.0 copy-start.2
  16.1 0.0 copy-start.3
  16.1 0.8 %finish_pages.1 = (bf16[32,256]{1,0:T(8,128)(2,1)S(1)}, bf16[32,256]{1,0:T(8,128)(2,1)S(1)}, bf16[32,256]{1,0:T(8,128)(2,1)S(1)}, bf16[32,256]{1,0:T(8,128)(2,1)S(1)}) custom-call(s32[7,9]{1,0:T(8,128)S(1)} %get-tuple-element.18.refs_4_.plan, bf16[128,128]{1,0:T(8,128)(2,1)S(1)} %get-tuple-element.26.pick, f32[80,128]{1,0:T(8,128)S(1)} %copy-done.1, ...), custom_call_target="tpu_custom_call" | custom-call | tf_op jit(solution)/shard_map/finish_pages/pallas_call | solution.py:436
  17.0 0.1 collective-permute-start.5
  17.0 1.6 %collective-permute-start.6 = (bf16[32,256]{1,0:T(8,128)(2,1)S(1)}, bf16[32,256]{1,0:T(8,128)(2,1)S(1)}, u32[]{:S(2)}, u32[]{:S(2)}) collective-permute-start(bf16[32,256]{1,0:T(8,128)(2,1)S(1)} %get-tuple-element.30), channel_id=1, source_target_pairs={{0,2},{1,3},{2,0},{3,1},{4,6},{5,7},{6,4},{7,5},{8,10},{9,11},{10,... | collective-permute-start | bytes 49160 | tf_op jit(solution)/shard_map/ppermute | solution.py:352
  18.6 1.4 %collective-permute-start.7 = (bf16[32,256]{1,0:T(8,128)(2,1)S(1)}, bf16[32,256]{1,0:T(8,128)(2,1)S(1)}, u32[]{:S(2)}, u32[]{:S(2)}) collective-permute-start(bf16[32,256]{1,0:T(8,128)(2,1)S(1)} %get-tuple-element.31), channel_id=1, source_target_pairs={{0,3},{1,0},{2,1},{3,2},{4,7},{5,4},{6,5},{7,6},{8,11},{9,8},{10,9... | collective-permute-start | bytes 49160 | tf_op jit(solution)/shard_map/ppermute | solution.py:352
  20.0 0.0 collective-permute-done.2.rest_1_
  20.0 0.7 %collective-permute-done.3.rest_2_ = bf16[10,8,512]{2,1,0:T(8,128)(2,1)S(1)} collective-permute-done((bf16[10,8,512]{2,1,0:T(8,128)(2,1)S(1)}, bf16[10,8,512]{2,1,0:T(8,128)(2,1)S(1)}, u32[]{:S(2)}, u32[]{:S(2)}) %collective-permute-start.3) | collective-permute-done | bytes 81952 | tf_op jit(solution)/shard_map/ppermute | solution.py:352
  20.7 2.3 %attention.1.rest_4_ = bf16[8,8,2048]{2,1,0:T(8,128)(2,1)} custom-call(s32[7,9]{1,0:T(8,128)S(1)} %get-tuple-element.18.refs_4_.plan, bf16[256,256]{1,0:T(8,128)(2,1)S(1)} %copy-done.2, bf16[256,256]{1,0:T(8,128)(2,1)S(1)} %copy-done.3, f32[80,128]{1,0:T(8,128)S(1)} %copy-done.1, f32[80,128]{1,0:T(8,128)S(1)} %copy-done, ...), custom_call_target="tpu_custom_call" | custom-call | tf_op jit(solution)/shard_map/attention/pallas_call | solution.py:450
  23.1 0.0 collective-permute-done.5.rest_1_
  23.1 0.0 collective-permute-done.6.rest_2_
  23.1 0.0 collective-permute-done.7.rest_3_
  23.1 0.7 %place_pages.1 = bf16[16,2,1024]{2,1,0:T(2,128)(2,1)} custom-call(bf16[32,256]{1,0:T(8,128)(2,1)S(1)} %get-tuple-element.28.rest_0_, bf16[32,256]{1,0:T(8,128)(2,1)S(1)} %collective-permute-done.5.rest_1_, bf16[32,256]{1,0:T(8,128)(2,1)S(1)} %collective-permute-done.6.rest_2_, bf16[32,256]{1,0:T(8,128)(2,1)S(1)} %collective-permute-done.7.rest_3_, ...), custom_call_target="tpu_custom_call" | custom-call | tf_op jit(solution)/shard_map/place_pages/pallas_call | solution.py:460
  (16 shorter events, 0.0 us)
Async XLA Ops:
  0.6 7.3 %copy-start.8 = (s32[4,4]{1,0:T(4,128)S(1)}, s32[4,4]{1,0:T(4,128)}, u32[]{:S(2)}) copy-start(s32[4,4]{1,0:T(4,128)} %page_start.1) | copy-start | bytes 196
  1.8 6.1 %copy-start.7 = (s32[4,4]{1,0:T(4,128)S(1)}, s32[4,4]{1,0:T(4,128)}, u32[]{:S(2)}) copy-start(s32[4,4]{1,0:T(4,128)} %prefix_len.1) | copy-start | bytes 196
  1.8 14.3 %collective-permute-start.4 = (bf16[14,8,512]{2,1,0:T(8,128)(2,1)S(1)}, bf16[14,8,512]{2,1,0:T(8,128)(2,1)S(1)}, u32[]{:S(2)}, u32[]{:S(2)}) collective-permute-start(bf16[14,8,512]{2,1,0:T(8,128)(2,1)S(1)} %get-tuple-element.25), channel_id=1, source_target_pairs={{0,12},{4,0},{8,4},{12,8},{1,13},{5,1},{9,5},{13,9},{2,14},{6,2},{... | collective-permute-start | bytes 344072 | tf_op jit(solution)/shard_map/ppermute | solution.py:352
  6.9 1.0 %copy-start.5 = (s32[4,4]{1,0:T(4,128)S(1)}, s32[4,4]{1,0:T(4,128)}, u32[]{:S(2)}) copy-start(s32[4,4]{1,0:T(4,128)} %owner.1) | copy-start | bytes 196
  6.9 1.0 %copy-start.4 = (s32[4,4]{1,0:T(4,128)S(1)}, s32[4,4]{1,0:T(4,128)}, u32[]{:S(2)}) copy-start(s32[4,4]{1,0:T(4,128)} %new_blocks.1) | copy-start | bytes 196
  6.9 5.7 %collective-permute-start = (bf16[4,8,512]{2,1,0:T(8,128)(2,1)S(1)}, bf16[4,8,512]{2,1,0:T(8,128)(2,1)S(1)}, u32[]{:S(2)}, u32[]{:S(2)}) collective-permute-start(bf16[4,8,512]{2,1,0:T(8,128)(2,1)S(1)} %get-tuple-element.21), channel_id=1, source_target_pairs={{0,4},{4,8},{8,12},{12,0},{1,5},{5,9},{9,13},{13,1},{2,6},{6,10},{... | collective-permute-start | bytes 98312 | tf_op jit(solution)/shard_map/ppermute | solution.py:352
  6.9 1.0 %copy-start.6 = (s32[4]{0:T(128)S(1)}, s32[4]{0:T(128)}, u32[]{:S(2)}) copy-start(s32[4]{0:T(128)} %spread.1) | copy-start | bytes 52
  6.9 5.7 %collective-permute-start.1 = (bf16[4,8,512]{2,1,0:T(8,128)(2,1)S(1)}, bf16[4,8,512]{2,1,0:T(8,128)(2,1)S(1)}, u32[]{:S(2)}, u32[]{:S(2)}) collective-permute-start(bf16[4,8,512]{2,1,0:T(8,128)(2,1)S(1)} %get-tuple-element.22), channel_id=1, source_target_pairs={{0,8},{4,12},{8,0},{12,4},{1,9},{5,13},{9,1},{13,5},{2,10},{6,14},... | collective-permute-start | bytes 98312 | tf_op jit(solution)/shard_map/ppermute | solution.py:352
  12.6 3.5 %copy-start = (f32[80,128]{1,0:T(8,128)S(1)}, f32[80,128]{1,0:T(8,128)}, u32[]{:S(2)}) copy-start(f32[80,128]{1,0:T(8,128)} %constant.5.clone.sine) | copy-start | bytes 122884
  12.6 3.5 %copy-start.1 = (f32[80,128]{1,0:T(8,128)S(1)}, f32[80,128]{1,0:T(8,128)}, u32[]{:S(2)}) copy-start(f32[80,128]{1,0:T(8,128)} %constant.4.clone.cosine) | copy-start | bytes 122884
  12.6 7.4 %collective-permute-start.2 = (bf16[10,8,512]{2,1,0:T(8,128)(2,1)S(1)}, bf16[10,8,512]{2,1,0:T(8,128)(2,1)S(1)}, u32[]{:S(2)}, u32[]{:S(2)}) collective-permute-start(bf16[10,8,512]{2,1,0:T(8,128)(2,1)S(1)} %get-tuple-element.23), channel_id=1, source_target_pairs={{0,4},{4,8},{8,12},{12,0},{1,5},{5,9},{9,13},{13,1},{2,6},{6,10},{... | collective-permute-start | bytes 245768 | tf_op jit(solution)/shard_map/ppermute | solution.py:352
  13.5 7.2 %collective-permute-start.3 = (bf16[10,8,512]{2,1,0:T(8,128)(2,1)S(1)}, bf16[10,8,512]{2,1,0:T(8,128)(2,1)S(1)}, u32[]{:S(2)}, u32[]{:S(2)}) collective-permute-start(bf16[10,8,512]{2,1,0:T(8,128)(2,1)S(1)} %get-tuple-element.24), channel_id=1, source_target_pairs={{0,8},{4,12},{8,0},{12,4},{1,9},{5,13},{9,1},{13,5},{2,10},{6,14},... | collective-permute-start | bytes 245768 | tf_op jit(solution)/shard_map/ppermute | solution.py:352
  16.1 4.6 %copy-start.2 = (bf16[256,256]{1,0:T(8,128)(2,1)S(1)}, bf16[256,256]{1,0:T(8,128)(2,1)}, u32[]{:S(2)}) copy-start(bf16[256,256]{1,0:T(8,128)(2,1)} %prefix_keys.1) | copy-start | bytes 393220
  16.1 4.6 %copy-start.3 = (bf16[256,256]{1,0:T(8,128)(2,1)S(1)}, bf16[256,256]{1,0:T(8,128)(2,1)}, u32[]{:S(2)}) copy-start(bf16[256,256]{1,0:T(8,128)(2,1)} %prefix_values.1) | copy-start | bytes 393220
  17.0 6.1 %collective-permute-start.5 = (bf16[32,256]{1,0:T(8,128)(2,1)S(1)}, bf16[32,256]{1,0:T(8,128)(2,1)S(1)}, u32[]{:S(2)}, u32[]{:S(2)}) collective-permute-start(bf16[32,256]{1,0:T(8,128)(2,1)S(1)} %get-tuple-element.29), channel_id=1, source_target_pairs={{0,1},{1,2},{2,3},{3,0},{4,5},{5,6},{6,7},{7,4},{8,9},{9,10},{10,1... | collective-permute-start | bytes 49160 | tf_op jit(solution)/shard_map/ppermute | solution.py:352
  17.0 6.0 %collective-permute-start.6 = (bf16[32,256]{1,0:T(8,128)(2,1)S(1)}, bf16[32,256]{1,0:T(8,128)(2,1)S(1)}, u32[]{:S(2)}, u32[]{:S(2)}) collective-permute-start(bf16[32,256]{1,0:T(8,128)(2,1)S(1)} %get-tuple-element.30), channel_id=1, source_target_pairs={{0,2},{1,3},{2,0},{3,1},{4,6},{5,7},{6,4},{7,5},{8,10},{9,11},{10,... | collective-permute-start | bytes 49160 | tf_op jit(solution)/shard_map/ppermute | solution.py:352
  18.6 4.5 %collective-permute-start.7 = (bf16[32,256]{1,0:T(8,128)(2,1)S(1)}, bf16[32,256]{1,0:T(8,128)(2,1)S(1)}, u32[]{:S(2)}, u32[]{:S(2)}) collective-permute-start(bf16[32,256]{1,0:T(8,128)(2,1)S(1)} %get-tuple-element.31), channel_id=1, source_target_pairs={{0,3},{1,0},{2,1},{3,2},{4,7},{5,4},{6,5},{7,6},{8,11},{9,8},{10,9... | collective-permute-start | bytes 49160 | tf_op jit(solution)/shard_map/ppermute | solution.py:352

commit v7 on v4

--- a/solution.py
+++ b/solution.py
@@ -277,8 +277,8 @@
             new_values[j] = here(width_q + width_k, width_k).astype(jnp.float32)
             blocks.append((j, here, cos, sin))
 
-    for at in range(0, len(blocks), 8):
-        some = blocks[at : at + 8]
+    for at in range(0, len(blocks), 4):
+        some = blocks[at : at + 4]
         for h in range(heads_k):
             part = slice(h * HEAD, (h + 1) * HEAD)
             scores = []

time: 22.5 us -> 23.1 us (1.027)
  Pallas kernels: 6.69 us -> 7.3 us
    pallas_call x1, Pallas kernels: 2.34 us -> 2.94 us  [per_device(): pl.pallas_call(functools.partial(attention_kernel, groups, heads_q, heads...]
  transfers between devices with their start and end apart: 8 -> 8, of which waited for: 3 -> 3; matrix products, arithmetic and copies ran while one was open for 0% -> 0% of each run, Pallas kernels for 22% -> 24%
where the time goes in v7:
time: 23.1 us; the launch traced here: 22.9 us
  starting transfers between devices  13.4 us (58%)
  Pallas kernels  7.3 us (32%)
  waiting for transfers between devices  1.41 us (6%)
  between operations  0.73 us (3%)
    ppermute x8, starting transfers between devices, shifted(): lax.ppermute(chunks[d], axis, [(i, (i + d) % size) for i in range(size)])  13.4 us
    pallas_call x1, Pallas kernels, per_device(): pl.pallas_call(functools.partial(attention_kernel, groups, heads_q, heads...  2.94 us
    pallas_call x1, Pallas kernels, per_device(): pl.pallas_call(functools.partial(plan_kernel, groups, tensors), out_shape...  1.72 us
    ppermute x8, waiting for transfers between devices, shifted(): lax.ppermute(chunks[d], axis, [(i, (i + d) % size) for i in range(size)])  1.41 us
    pallas_call x1, Pallas kernels, per_device(): pl.pallas_call(functools.partial(dispatch_kernel, groups), out_shape=[chu...  1.11 us
    pallas_call x1, Pallas kernels, per_device(): pl.pallas_call(functools.partial(pages_kernel, groups, tensors), out_shap...  0.83 us
    pallas_call x1, Pallas kernels, per_device(): pl.pallas_call(functools.partial(cache_kernel, tensors), out_shape=jax.Sh...  0.69 us
  transfers between devices with their start and end apart: 8, of which 3 were waited for; matrix products, arithmetic and copies ran while one was open for 0% of the time, Pallas kernels for 24%

profile of v7, /device:TPU:0, one launch (start us, length us, event | category | flops | bytes accessed | tf_op | source)
XLA Modules:
  0.0 22.9 jit_solution(9002977707269595899)
XLA Ops:
  0.6 1.1 %dispatch.1 = (bf16[10,8,512]{2,1,0:T(8,128)(2,1)S(1)}, bf16[14,8,512]{2,1,0:T(8,128)(2,1)S(1)}, bf16[10,8,512]{2,1,0:T(8,128)(2,1)S(1)}, bf16[10,8,512]{2,1,0:T...) custom-call(s32[4]{0:T(128)} %spread.1, ...), custom_call_target="tpu_custom_call" | custom-call | tf_op jit(solution)/shard_map/dispatch/pallas_call | solution.py:393
  1.8 0.0 copy-start.7
  1.8 3.1 %collective-permute-start = (bf16[14,8,512]{2,1,0:T(8,128)(2,1)S(1)}, bf16[14,8,512]{2,1,0:T(8,128)(2,1)S(1)}, u32[]{:S(2)}, u32[]{:S(2)}) collective-permute-start(bf16[14,8,512]{2,1,0:T(8,128)(2,1)S(1)} %get-tuple-element.19), channel_id=1, source_target_pairs={{0,4},{4,8},{8,12},{12,0},{1,5},{5,9},{9,13},{13,1},{2,6},{6,10},{... | collective-permute-start | bytes 344072 | tf_op jit(solution)/shard_map/ppermute | solution.py:352
  4.9 2.6 %collective-permute-start.1 = (bf16[4,8,512]{2,1,0:T(8,128)(2,1)S(1)}, bf16[4,8,512]{2,1,0:T(8,128)(2,1)S(1)}, u32[]{:S(2)}, u32[]{:S(2)}) collective-permute-start(bf16[4,8,512]{2,1,0:T(8,128)(2,1)S(1)} %get-tuple-element.22), channel_id=1, source_target_pairs={{0,8},{4,12},{8,0},{12,4},{1,9},{5,13},{9,1},{13,5},{2,10},{6,14},... | collective-permute-start | bytes 98312 | tf_op jit(solution)/shard_map/ppermute | solution.py:352
  7.4 1.3 %collective-permute-start.2 = (bf16[4,8,512]{2,1,0:T(8,128)(2,1)S(1)}, bf16[4,8,512]{2,1,0:T(8,128)(2,1)S(1)}, u32[]{:S(2)}, u32[]{:S(2)}) collective-permute-start(bf16[4,8,512]{2,1,0:T(8,128)(2,1)S(1)} %get-tuple-element.23), channel_id=1, source_target_pairs={{0,12},{4,0},{8,4},{12,8},{1,13},{5,1},{9,5},{13,9},{2,14},{6,2},{... | collective-permute-start | bytes 98312 | tf_op jit(solution)/shard_map/ppermute | solution.py:352
  8.8 1.7 %plan.1 = (s32[7,9]{1,0:T(8,128)S(1)}, bf16[128,128]{1,0:T(8,128)(2,1)S(1)}) custom-call(s32[4]{0:T(128)S(1)} %copy-done.6, s32[4,4]{1,0:T(4,128)S(1)} %copy-done.4, s32[4,4]{1,0:T(4,128)S(1)} %copy-done.7, s32[4,4]{1,0:T(4,128)S(1)} %copy-done.5, s32[4,4]{1,0:T(4,128)S(1)} %copy-done.8, bf16[10,8,512]{2,1,0:T(8,128)(2,1)S(1)} %get-tuple-element.17._.rest_0_), custom_call_target="tpu_custom_call" | custom-call | tf_op jit(solution)/shard_map/plan/pallas_call | solution.py:416
  10.5 1.0 %collective-permute-done.1.refs_2_.rest_2_ = bf16[4,8,512]{2,1,0:T(8,128)(2,1)S(1)} collective-permute-done((bf16[4,8,512]{2,1,0:T(8,128)(2,1)S(1)}, bf16[4,8,512]{2,1,0:T(8,128)(2,1)S(1)}, u32[]{:S(2)}, u32[]{:S(2)}) %collective-permute-start.1) | collective-permute-done | bytes 32800 | tf_op jit(solution)/shard_map/ppermute | solution.py:352
  11.5 0.1 collective-permute-done.2.refs_3_.rest_3_
  11.7 0.8 %collective-permute-start.3 = (bf16[10,8,512]{2,1,0:T(8,128)(2,1)S(1)}, bf16[10,8,512]{2,1,0:T(8,128)(2,1)S(1)}, u32[]{:S(2)}, u32[]{:S(2)}) collective-permute-start(bf16[10,8,512]{2,1,0:T(8,128)(2,1)S(1)} %get-tuple-element.24), channel_id=1, source_target_pairs={{0,8},{4,12},{8,0},{12,4},{1,9},{5,13},{9,1},{13,5},{2,10},{6,14},... | collective-permute-start | bytes 245768 | tf_op jit(solution)/shard_map/ppermute | solution.py:352
  12.4 2.6 %collective-permute-start.4 = (bf16[10,8,512]{2,1,0:T(8,128)(2,1)S(1)}, bf16[10,8,512]{2,1,0:T(8,128)(2,1)S(1)}, u32[]{:S(2)}, u32[]{:S(2)}) collective-permute-start(bf16[10,8,512]{2,1,0:T(8,128)(2,1)S(1)} %get-tuple-element.25), channel_id=1, source_target_pairs={{0,12},{4,0},{8,4},{12,8},{1,13},{5,1},{9,5},{13,9},{2,14},{6,2},{... | collective-permute-start | bytes 245768 | tf_op jit(solution)/shard_map/ppermute | solution.py:352
  15.1 0.0 collective-permute-done.rest_1_
  15.1 0.0 copy-start.2
  15.1 0.0 copy-start.3
  15.1 0.8 %finish_pages.1 = (bf16[32,256]{1,0:T(8,128)(2,1)S(1)}, bf16[32,256]{1,0:T(8,128)(2,1)S(1)}, bf16[32,256]{1,0:T(8,128)(2,1)S(1)}, bf16[32,256]{1,0:T(8,128)(2,1)S(1)}) custom-call(s32[7,9]{1,0:T(8,128)S(1)} %get-tuple-element.18.refs_4_.plan, bf16[128,128]{1,0:T(8,128)(2,1)S(1)} %get-tuple-element.26.pick, f32[80,128]{1,0:T(8,128)S(1)} %copy-done.1, ...), custom_call_target="tpu_custom_call" | custom-call | tf_op jit(solution)/shard_map/finish_pages/pallas_call | solution.py:436
  15.9 0.1 collective-permute-start.5
  16.0 1.6 %collective-permute-start.6 = (bf16[32,256]{1,0:T(8,128)(2,1)S(1)}, bf16[32,256]{1,0:T(8,128)(2,1)S(1)}, u32[]{:S(2)}, u32[]{:S(2)}) collective-permute-start(bf16[32,256]{1,0:T(8,128)(2,1)S(1)} %get-tuple-element.30), channel_id=1, source_target_pairs={{0,2},{1,3},{2,0},{3,1},{4,6},{5,7},{6,4},{7,5},{8,10},{9,11},{10,... | collective-permute-start | bytes 49160 | tf_op jit(solution)/shard_map/ppermute | solution.py:352
  17.6 1.4 %collective-permute-start.7 = (bf16[32,256]{1,0:T(8,128)(2,1)S(1)}, bf16[32,256]{1,0:T(8,128)(2,1)S(1)}, u32[]{:S(2)}, u32[]{:S(2)}) collective-permute-start(bf16[32,256]{1,0:T(8,128)(2,1)S(1)} %get-tuple-element.31), channel_id=1, source_target_pairs={{0,3},{1,0},{2,1},{3,2},{4,7},{5,4},{6,5},{7,6},{8,11},{9,8},{10,9... | collective-permute-start | bytes 49160 | tf_op jit(solution)/shard_map/ppermute | solution.py:352
  19.0 0.3 %collective-permute-done.3.rest_2_ = bf16[10,8,512]{2,1,0:T(8,128)(2,1)S(1)} collective-permute-done((bf16[10,8,512]{2,1,0:T(8,128)(2,1)S(1)}, bf16[10,8,512]{2,1,0:T(8,128)(2,1)S(1)}, u32[]{:S(2)}, u32[]{:S(2)}) %collective-permute-start.3) | collective-permute-done | bytes 81952 | tf_op jit(solution)/shard_map/ppermute | solution.py:352
  19.3 0.0 collective-permute-done.4.rest_3_
  19.3 2.9 %attention.1.rest_4_ = bf16[8,8,2048]{2,1,0:T(8,128)(2,1)} custom-call(s32[7,9]{1,0:T(8,128)S(1)} %get-tuple-element.18.refs_4_.plan, bf16[256,256]{1,0:T(8,128)(2,1)S(1)} %copy-done.2, bf16[256,256]{1,0:T(8,128)(2,1)S(1)} %copy-done.3, f32[80,128]{1,0:T(8,128)S(1)} %copy-done.1, f32[80,128]{1,0:T(8,128)S(1)} %copy-done, ...), custom_call_target="tpu_custom_call" | custom-call | tf_op jit(solution)/shard_map/attention/pallas_call | solution.py:450
  22.2 0.0 collective-permute-done.5.rest_1_
  22.2 0.0 collective-permute-done.6.rest_2_
  22.2 0.0 collective-permute-done.7.rest_3_
  22.2 0.7 %place_pages.1 = bf16[16,2,1024]{2,1,0:T(2,128)(2,1)} custom-call(bf16[32,256]{1,0:T(8,128)(2,1)S(1)} %get-tuple-element.28.rest_0_, bf16[32,256]{1,0:T(8,128)(2,1)S(1)} %collective-permute-done.5.rest_1_, bf16[32,256]{1,0:T(8,128)(2,1)S(1)} %collective-permute-done.6.rest_2_, bf16[32,256]{1,0:T(8,128)(2,1)S(1)} %collective-permute-done.7.rest_3_, ...), custom_call_target="tpu_custom_call" | custom-call | tf_op jit(solution)/shard_map/place_pages/pallas_call | solution.py:460
  (16 shorter events, 0.0 us)
Async XLA Ops:
  0.6 8.2 %copy-start.8 = (s32[4,4]{1,0:T(4,128)S(1)}, s32[4,4]{1,0:T(4,128)}, u32[]{:S(2)}) copy-start(s32[4,4]{1,0:T(4,128)} %page_start.1) | copy-start | bytes 196
  1.8 7.0 %copy-start.7 = (s32[4,4]{1,0:T(4,128)S(1)}, s32[4,4]{1,0:T(4,128)}, u32[]{:S(2)}) copy-start(s32[4,4]{1,0:T(4,128)} %prefix_len.1) | copy-start | bytes 196
  1.8 13.3 %collective-permute-start = (bf16[14,8,512]{2,1,0:T(8,128)(2,1)S(1)}, bf16[14,8,512]{2,1,0:T(8,128)(2,1)S(1)}, u32[]{:S(2)}, u32[]{:S(2)}) collective-permute-start(bf16[14,8,512]{2,1,0:T(8,128)(2,1)S(1)} %get-tuple-element.19), channel_id=1, source_target_pairs={{0,4},{4,8},{8,12},{12,0},{1,5},{5,9},{9,13},{13,1},{2,6},{6,10},{... | collective-permute-start | bytes 344072 | tf_op jit(solution)/shard_map/ppermute | solution.py:352
  4.9 4.0 %copy-start.5 = (s32[4,4]{1,0:T(4,128)S(1)}, s32[4,4]{1,0:T(4,128)}, u32[]{:S(2)}) copy-start(s32[4,4]{1,0:T(4,128)} %owner.1) | copy-start | bytes 196
  4.9 4.0 %copy-start.4 = (s32[4,4]{1,0:T(4,128)S(1)}, s32[4,4]{1,0:T(4,128)}, u32[]{:S(2)}) copy-start(s32[4,4]{1,0:T(4,128)} %new_blocks.1) | copy-start | bytes 196
  4.9 6.7 %collective-permute-start.1 = (bf16[4,8,512]{2,1,0:T(8,128)(2,1)S(1)}, bf16[4,8,512]{2,1,0:T(8,128)(2,1)S(1)}, u32[]{:S(2)}, u32[]{:S(2)}) collective-permute-start(bf16[4,8,512]{2,1,0:T(8,128)(2,1)S(1)} %get-tuple-element.22), channel_id=1, source_target_pairs={{0,8},{4,12},{8,0},{12,4},{1,9},{5,13},{9,1},{13,5},{2,10},{6,14},... | collective-permute-start | bytes 98312 | tf_op jit(solution)/shard_map/ppermute | solution.py:352
  7.4 1.4 %copy-start.6 = (s32[4]{0:T(128)S(1)}, s32[4]{0:T(128)}, u32[]{:S(2)}) copy-start(s32[4]{0:T(128)} %spread.1) | copy-start | bytes 52
  7.4 4.2 %collective-permute-start.2 = (bf16[4,8,512]{2,1,0:T(8,128)(2,1)S(1)}, bf16[4,8,512]{2,1,0:T(8,128)(2,1)S(1)}, u32[]{:S(2)}, u32[]{:S(2)}) collective-permute-start(bf16[4,8,512]{2,1,0:T(8,128)(2,1)S(1)} %get-tuple-element.23), channel_id=1, source_target_pairs={{0,12},{4,0},{8,4},{12,8},{1,13},{5,1},{9,5},{13,9},{2,14},{6,2},{... | collective-permute-start | bytes 98312 | tf_op jit(solution)/shard_map/ppermute | solution.py:352
  11.7 3.4 %copy-start = (f32[80,128]{1,0:T(8,128)S(1)}, f32[80,128]{1,0:T(8,128)}, u32[]{:S(2)}) copy-start(f32[80,128]{1,0:T(8,128)} %constant.5.clone.sine) | copy-start | bytes 122884
  11.7 3.4 %copy-start.1 = (f32[80,128]{1,0:T(8,128)S(1)}, f32[80,128]{1,0:T(8,128)}, u32[]{:S(2)}) copy-start(f32[80,128]{1,0:T(8,128)} %constant.4.clone.cosine) | copy-start | bytes 122884
  11.7 7.6 %collective-permute-start.3 = (bf16[10,8,512]{2,1,0:T(8,128)(2,1)S(1)}, bf16[10,8,512]{2,1,0:T(8,128)(2,1)S(1)}, u32[]{:S(2)}, u32[]{:S(2)}) collective-permute-start(bf16[10,8,512]{2,1,0:T(8,128)(2,1)S(1)} %get-tuple-element.24), channel_id=1, source_target_pairs={{0,8},{4,12},{8,0},{12,4},{1,9},{5,13},{9,1},{13,5},{2,10},{6,14},... | collective-permute-start | bytes 245768 | tf_op jit(solution)/shard_map/ppermute | solution.py:352
  12.4 6.8 %collective-permute-start.4 = (bf16[10,8,512]{2,1,0:T(8,128)(2,1)S(1)}, bf16[10,8,512]{2,1,0:T(8,128)(2,1)S(1)}, u32[]{:S(2)}, u32[]{:S(2)}) collective-permute-start(bf16[10,8,512]{2,1,0:T(8,128)(2,1)S(1)} %get-tuple-element.25), channel_id=1, source_target_pairs={{0,12},{4,0},{8,4},{12,8},{1,13},{5,1},{9,5},{13,9},{2,14},{6,2},{... | collective-permute-start | bytes 245768 | tf_op jit(solution)/shard_map/ppermute | solution.py:352
  15.1 4.2 %copy-start.2 = (bf16[256,256]{1,0:T(8,128)(2,1)S(1)}, bf16[256,256]{1,0:T(8,128)(2,1)}, u32[]{:S(2)}) copy-start(bf16[256,256]{1,0:T(8,128)(2,1)} %prefix_keys.1) | copy-start | bytes 393220
  15.1 4.2 %copy-start.3 = (bf16[256,256]{1,0:T(8,128)(2,1)S(1)}, bf16[256,256]{1,0:T(8,128)(2,1)}, u32[]{:S(2)}) copy-start(bf16[256,256]{1,0:T(8,128)(2,1)} %prefix_values.1) | copy-start | bytes 393220
  15.9 6.3 %collective-permute-start.5 = (bf16[32,256]{1,0:T(8,128)(2,1)S(1)}, bf16[32,256]{1,0:T(8,128)(2,1)S(1)}, u32[]{:S(2)}, u32[]{:S(2)}) collective-permute-start(bf16[32,256]{1,0:T(8,128)(2,1)S(1)} %get-tuple-element.29), channel_id=1, source_target_pairs={{0,1},{1,2},{2,3},{3,0},{4,5},{5,6},{6,7},{7,4},{8,9},{9,10},{10,1... | collective-permute-start | bytes 49160 | tf_op jit(solution)/shard_map/ppermute | solution.py:352
  16.0 6.2 %collective-permute-start.6 = (bf16[32,256]{1,0:T(8,128)(2,1)S(1)}, bf16[32,256]{1,0:T(8,128)(2,1)S(1)}, u32[]{:S(2)}, u32[]{:S(2)}) collective-permute-start(bf16[32,256]{1,0:T(8,128)(2,1)S(1)} %get-tuple-element.30), channel_id=1, source_target_pairs={{0,2},{1,3},{2,0},{3,1},{4,6},{5,7},{6,4},{7,5},{8,10},{9,11},{10,... | collective-permute-start | bytes 49160 | tf_op jit(solution)/shard_map/ppermute | solution.py:352
  17.6 4.6 %collective-permute-start.7 = (bf16[32,256]{1,0:T(8,128)(2,1)S(1)}, bf16[32,256]{1,0:T(8,128)(2,1)S(1)}, u32[]{:S(2)}, u32[]{:S(2)}) collective-permute-start(bf16[32,256]{1,0:T(8,128)(2,1)S(1)} %get-tuple-element.31), channel_id=1, source_target_pairs={{0,3},{1,0},{2,1},{3,2},{4,7},{5,4},{6,5},{7,6},{8,11},{9,8},{10,9... | collective-permute-start | bytes 49160 | tf_op jit(solution)/shard_map/ppermute | solution.py:352
